TPU v7x, 32 devices: a whole 2x2x4 slice. The times are simulated.
32 devices in a mesh: row: 8 (over y, x, core), col: 4 (over z).
Axes of the slice: x: 2, y: 2, z: 4, core: 2. Of those that a mesh axis runs over, the one named last changes fastest.
Arguments:
- activations: bfloat16 [256, 16384], P('col', 'row'), may hold values from -6 to 6
- grad_out: bfloat16 [256, 16384], P('col', 'row'), may hold values from -1.5 to 1.5
- first_blocks: bfloat16 [8, 4, 384, 128, 128], P('row', 'col'), may hold values from -0.125 to 0.125
- first_coords: int32 [8, 4, 384, 2], P('row', 'col'), may hold values from -1 to 511, as said below
- second_blocks: bfloat16 [4, 8, 384, 128, 128], P('col', 'row'), may hold values from -0.0625 to 0.0625
- second_coords: int32 [4, 8, 384, 2], P('col', 'row'), may hold values from -1 to 511, as said below
Outputs:
- output: float32 [256, 16384], P('col', 'row')
- grad_input: float32 [256, 16384], P('col', 'row')
- grad_first: bfloat16 [8, 4, 384, 128, 128], P('row', 'col')
- grad_second: bfloat16 [4, 8, 384, 128, 128], P('col', 'row')
Inputs may be any that keep to these rules, and one draw needn't show every extreme that they name: `first_coords`: tile [a, b] lists, once each, exactly the nonzero blocks of W1 whose block row lies in a * 16 to a * 16 + 15 and whose block column lies in b * 128 to b * 128 + 127, in increasing order of block row and then block column; the remaining of its 384 slots hold -1 in both coordinates. Some tile fills all 384 slots. `second_coords`: tile [a, b] lists, once each, exactly the nonzero blocks of W2 whose block row lies in a * 128 to a * 128 + 127 and whose block column lies in b * 16 to b * 16 + 15, in increasing order of block row and then block column; the remaining of its 384 slots hold -1 in both coordinates. Some tile fills all 384 slots.
All inputs are finite; a program needn't handle non-finite values.
Results may differ from a plain program's by a relative error of at most 0.005.
Values may be sent and summed in bfloat16 or wider, within the bound.
A program may use at most 320 MiB of HBM per device.

v0:
```python
import jax
import jax.numpy as jnp
from jax import lax
from jax.sharding import PartitionSpec as P

FF = 65536


def gelu_tanh(values):
    return jax.nn.gelu(values, approximate=True)


def slot_fields(coords, row_base, col_base):
    block_rows = coords[0, 0, :, 0]
    block_cols = coords[0, 0, :, 1]
    is_live = block_rows >= 0
    local_rows = jnp.where(is_live, block_rows - row_base, 0)
    local_cols = jnp.where(is_live, block_cols - col_base, 0)
    return (is_live, local_rows, local_cols)


def sparse_apply(panels, blocks, source, target, is_live, segments, flipped):
    token_count = panels.shape[0]
    block_width = blocks.shape[-1]
    block_grid = panels.reshape(token_count, -1, block_width)
    picked = jnp.take(block_grid, source, axis=1)
    if flipped:
        products = jnp.einsum("rsk,snk->srn", picked, blocks, preferred_element_type=jnp.float32)
    else:
        products = jnp.einsum("rsk,skn->srn", picked, blocks, preferred_element_type=jnp.float32)
    targets = jnp.where(is_live, target, segments)
    summed = jax.ops.segment_sum(products, targets, num_segments=segments + 1)[:segments]
    return jnp.transpose(summed, (1, 0, 2)).reshape(token_count, segments * block_width)


def block_grads(left, right, left_source, right_source, is_live, block_width):
    token_count = left.shape[0]
    picked_left = jnp.take(left.reshape(token_count, -1, block_width), left_source, axis=1)
    picked_right = jnp.take(right.reshape(token_count, -1, block_width), right_source, axis=1)
    grads = jnp.einsum(
        "rsk,rsn->skn", picked_left, picked_right, preferred_element_type=jnp.float32
    )
    grads = jnp.where(is_live[:, None, None], grads, 0.0)
    return grads.astype(jnp.bfloat16)[None, None]


def body(activations, grad_out, first_blocks, first_coords, second_blocks, second_coords):
    block_width = first_blocks.shape[-1]
    row_tiles = activations.shape[1] // block_width
    col_tiles = FF // block_width // lax.axis_size("col")
    row_index = lax.axis_index("row")
    col_index = lax.axis_index("col")
    live_one, model_one, hidden_one = slot_fields(
        first_coords, row_index * row_tiles, col_index * col_tiles
    )
    live_two, hidden_two, model_two = slot_fields(
        second_coords, col_index * col_tiles, row_index * row_tiles
    )
    weights_one = first_blocks[0, 0]
    weights_two = second_blocks[0, 0]
    inputs_all, cotangent_all = (
        lax.all_gather(activations, "col", axis=0, tiled=True),
        lax.all_gather(grad_out, "col", axis=0, tiled=True),
    )
    pre_terms = sparse_apply(
        inputs_all, weights_one, model_one, hidden_one, live_one, col_tiles, False
    )
    pre_all = lax.psum(pre_terms, "row")
    hidden_full, gelu_back = jax.vjp(gelu_tanh, pre_all)
    hidden_all = hidden_full.astype(jnp.bfloat16)
    back_terms = sparse_apply(
        cotangent_all, weights_two, model_two, hidden_two, live_two, col_tiles, True
    )
    grad_hidden = lax.psum(back_terms, "row")
    grad_pre_all = gelu_back(grad_hidden)[0].astype(jnp.bfloat16)
    output = lax.psum_scatter(
        sparse_apply(hidden_all, weights_two, hidden_two, model_two, live_two, row_tiles, False),
        "col",
        scatter_dimension=0,
        tiled=True,
    )
    grad_input = lax.psum_scatter(
        sparse_apply(grad_pre_all, weights_one, hidden_one, model_one, live_one, row_tiles, True),
        "col",
        scatter_dimension=0,
        tiled=True,
    )
    grad_first = block_grads(inputs_all, grad_pre_all, model_one, hidden_one, live_one, block_width)
    grad_second = block_grads(
        hidden_all, cotangent_all, hidden_two, model_two, live_two, block_width
    )
    return (output, grad_input, grad_first, grad_second)


def solution(mesh):
    return jax.shard_map(
        body,
        mesh=mesh,
        in_specs=(
            P("col", "row"),
            P("col", "row"),
            P("row", "col", None, None, None),
            P("row", "col", None, None),
            P("col", "row", None, None, None),
            P("col", "row", None, None),
        ),
        out_specs=(
            P("col", "row"),
            P("col", "row"),
            P("row", "col", None, None, None),
            P("col", "row", None, None, None),
        ),
        check_vma=False,
    )
```

profile of v0, /device:TPU:0, one launch (start us, length us, event | category | flops | bytes accessed | tf_op | source)
XLA Modules:
  0.0 1210.7 jit_solution(4917931830340449708)
XLA Ops:
  13.5 26.7 %all-gather.3.cloned.1.call-done = bf16[256,2048]{1,0:T(8,128)(2,1)} async-done(((bf16[64,2048]{1,0:T(8,128)(2,1)}), bf16[256,2048]{1,0:T(8,128)(2,1)}) %all-gather.3.cloned.1.call-update) | async-done | bytes 1048592 | tf_op jit(solution)/shard_map/all_gather | solution.py:62
  42.4 26.9 %all-gather.5.cloned.1.call-done = bf16[256,2048]{1,0:T(8,128)(2,1)} async-done(((bf16[64,2048]{1,0:T(8,128)(2,1)}), bf16[256,2048]{1,0:T(8,128)(2,1)}) %all-gather.5.cloned.1.call-update) | async-done | bytes 1048592 | tf_op jit(solution)/shard_map/all_gather | solution.py:63
  71.4 12.7 %gather_fusion.2 = bf16[384,256,128]{2,1,0:T(8,128)(2,1)} fusion(bf16[256,16,128]{2,0,1:T(8,128)(2,1)S(1)} %copy.34, s32[1024]{0:T(1024)S(1)} %pad_clamp_fusion.1), kind=kCustom, calls=%fused_computation.2.clone | custom fusion | bytes 50333184 | tf_op jit(solution)/shard_map/jit(_take)/gather | solution.py:26
  84.2 31.6 %fusion.6 = f32[384,256,128]{2,1,0:T(8,128)} fusion(bf16[1,1,384,128,128]{4,3,2,1,0:T(8,128)(2,1)} %param.14, bf16[384,256,128]{2,1,0:T(8,128)(2,1)} %gather_fusion.2, pred[384]{0:T(512)(128)(4,1)S(1)} %get-tuple-element.36), kind=kOutput, calls=%fused_computation.14 | convolution fusion | flops 3233808384 | bytes 88080768 | tf_op jit(solution)/shard_map/rsk,snk->srn/dot_general | solution.py:28
  123.6 106.8 %scatter_fusion.2 = f32[129,256,128]{2,1,0:T(8,128)} fusion(f32[129,256,128]{2,1,0:T(8,128)} %broadcast.167.clone.1, s32[384]{0:T(512)S(1)} %get-tuple-element.18, f32[384,256,128]{2,1,0:T(8,128)} %fusion.6), kind=kCustom, calls=%fused_computation.6 | custom fusion | flops 12582912 | bytes 150996480 | tf_op jit(solution)/shard_map/scatter-add | solution.py:32
  230.5 11.6 slice_bitcast_fusion
  242.1 17.4 %copy.35 = f32[256,128,128]{0,2,1:T(8,128)} copy(f32[256,128,128]{2,0,1:T(8,128)} %slice_bitcast_fusion) | data formatting | bytes 33554432 | tf_op jit(solution)/shard_map/transpose | solution.py:33
  259.5 12.0 gather_fusion
  271.5 30.1 %fusion.12 = f32[384,256,128]{2,1,0:T(8,128)} fusion(bf16[1,1,384,128,128]{4,3,2,1,0:T(8,128)(2,1)} %param.12, bf16[384,256,128]{2,1,0:T(8,128)(2,1)} %gather_fusion, pred[384]{0:T(512)(128)(4,1)S(1)} %get-tuple-element.34), kind=kOutput, calls=%fused_computation.20 | convolution fusion | flops 3233808384 | bytes 88080768 | tf_op jit(solution)/shard_map/rsk,skn->srn/dot_general | solution.py:30
  309.5 115.9 %scatter_fusion = f32[129,256,128]{2,1,0:T(8,128)} fusion(f32[129,256,128]{2,1,0:T(8,128)} %broadcast.167.clone, s32[384]{0:T(512)S(1)} %copy-done.9, f32[384,256,128]{2,1,0:T(8,128)} %fusion.12), kind=kCustom, calls=%fused_computation.4 | custom fusion | flops 12582912 | bytes 150996480 | tf_op jit(solution)/shard_map/scatter-add | solution.py:32
  425.4 11.5 slice_bitcast_fusion.1
  437.0 17.4 %copy.30 = f32[256,128,128]{0,2,1:T(8,128)} copy(f32[256,128,128]{2,0,1:T(8,128)} %slice_bitcast_fusion.1) | data formatting | bytes 33554432 | tf_op jit(solution)/shard_map/transpose | solution.py:33
  455.1 409.7 %all-reduce.3.cloned.1.call-done = (f32[256,16384]{0,1:T(8,128)}, f32[256,16384]{0,1:T(8,128)}) async-done(((f32[256,16384]{0,1:T(8,128)}, f32[256,16384]{0,1:T(8,128)}), (f32[256,16384]{0,1:T(8,128)}, f32[256,16384]{0,1:T(8,128)})) %all-reduce.3.cloned.1.call-update) | async-done | bytes 33554448 | tf_op jit(solution)/shard_map/psum | solution.py:68
  864.7 20.9 %fusion.20 = (bf16[256,16384]{0,1:T(8,128)(2,1)}, bf16[256,16384]{0,1:T(8,128)(2,1)}) fusion(f32[256,16384]{0,1:T(8,128)} %get-tuple-element.22, f32[256,16384]{0,1:T(8,128)} %get-tuple-element.23), kind=kLoop, calls=%fused_computation.36 | loop fusion | flops 92274688 | bytes 50331648 | tf_op jit(solution)/shard_map/convert_element_type | solution.py:75
  885.6 11.9 copy.36
  897.6 15.4 %gather_fusion.3 = bf16[384,256,128]{2,1,0:T(8,128)(2,1)} fusion(bf16[256,128,128]{2,0,1:T(8,128)(2,1)} %copy.36, s32[1024]{0:T(1024)S(1)} %pad_clamp_fusion), kind=kCustom, calls=%fused_computation.3.clone | custom fusion | bytes 50333184 | tf_op jit(solution)/shard_map/jit(_take)/gather | solution.py:26
  913.0 31.6 %fusion.2 = f32[384,256,128]{2,1,0:T(8,128)} fusion(bf16[1,1,384,128,128]{4,3,2,1,0:T(8,128)(2,1)} %param.12, bf16[384,256,128]{2,1,0:T(8,128)(2,1)} %gather_fusion.3, pred[384]{0:T(512)(128)(4,1)S(1)} %copy-done.3), kind=kOutput, calls=%fused_computation.10 | convolution fusion | flops 3233808384 | bytes 88080768 | tf_op jit(solution)/shard_map/rsk,snk->srn/dot_general | solution.py:28
  944.8 71.0 %scatter_fusion.3 = f32[17,256,128]{2,1,0:T(8,128)S(1)} fusion(f32[17,256,128]{2,1,0:T(8,128)S(1)} %broadcast.164.clone.1, s32[384]{0:T(512)S(1)} %copy-done.8, f32[384,256,128]{2,1,0:T(8,128)} %fusion.2), kind=kCustom, calls=%fused_computation.7 | custom fusion | flops 12582912 | bytes 150996480 | tf_op jit(solution)/shard_map/scatter-add | solution.py:32
  1021.2 12.2 %copy.31 = bf16[256,128,128]{2,0,1:T(8,128)(2,1)} copy(bf16[256,128,128]{0,2,1:T(8,128)(2,1)} %bitcast.96) | data formatting | bytes 16777216 | tf_op jit(solution)/shard_map/reshape | solution.py:25
  1033.3 16.4 %gather_fusion.1 = bf16[384,256,128]{2,1,0:T(8,128)(2,1)} fusion(bf16[256,128,128]{2,0,1:T(8,128)(2,1)} %copy.31, s32[1024]{0:T(1024)S(1)} %pad_clamp_fusion.2), kind=kCustom, calls=%fused_computation.1.clone | custom fusion | bytes 50333184 | tf_op jit(solution)/shard_map/jit(_take)/gather | solution.py:26
  1049.7 30.0 %fusion.9 = f32[384,256,128]{2,1,0:T(8,128)} fusion(bf16[1,1,384,128,128]{4,3,2,1,0:T(8,128)(2,1)} %param.14, bf16[384,256,128]{2,1,0:T(8,128)(2,1)} %gather_fusion.1, pred[384]{0:T(512)(128)(4,1)S(1)} %copy-done), kind=kOutput, calls=%fused_computation.17 | convolution fusion | flops 3233808384 | bytes 88080768 | tf_op jit(solution)/shard_map/rsk,skn->srn/dot_general | solution.py:30
  1080.0 71.5 %scatter_fusion.1 = f32[17,256,128]{2,1,0:T(8,128)S(1)} fusion(f32[17,256,128]{2,1,0:T(8,128)S(1)} %broadcast.164.clone, s32[384]{0:T(512)S(1)} %copy-done.7, f32[384,256,128]{2,1,0:T(8,128)} %fusion.9), kind=kCustom, calls=%fused_computation.5 | custom fusion | flops 12582912 | bytes 150996480 | tf_op jit(solution)/shard_map/scatter-add | solution.py:32
  1156.9 23.2 %fusion.22 = bf16[1,1,384,128,128]{4,3,2,1,0:T(8,128)(2,1)} fusion(pred[384]{0:T(512)(128)(4,1)S(1)} %copy-done.13, bf16[384,256,128]{2,1,0:T(8,128)(2,1)} %gather_fusion.2, pred[384]{0:T(512)(128)(4,1)S(1)} %copy-done.2, bf16[384,256,128]{2,1,0:T(8,128)(2,1)} %gather_fusion.1, pred[384]{0:T(512)(128)(4,1)S(1)} %copy-done), kind=kOutput, calls=%fused_computation.41 | convolution fusion | flops 3258974208 | bytes 62915712 | tf_op jit(solution)/shard_map/rsk,rsn->skn/dot_general | solution.py:40
  1180.1 23.6 %fusion.21 = bf16[1,1,384,128,128]{4,3,2,1,0:T(8,128)(2,1)} fusion(pred[384]{0:T(512)(128)(4,1)S(1)} %copy-done.15, bf16[384,256,128]{2,1,0:T(8,128)(2,1)} %gather_fusion.3, pred[384]{0:T(512)(128)(4,1)S(1)} %copy-done.4, bf16[384,256,128]{2,1,0:T(8,128)(2,1)} %gather_fusion, pred[384]{0:T(512)(128)(4,1)S(1)} %copy-done.6), kind=kOutput, calls=%fused_computation.40 | convolution fusion | flops 3258974208 | bytes 62915712 | tf_op jit(solution)/shard_map/rsk,rsn->skn/dot_general | solution.py:40
  (68 shorter events, 38.1 us)
Async XLA Ops:
  7.2 33.1 %all-gather.3.cloned.1.call-start = ((), (), s32[]{:S(2)}) async-start(), calls=%async_computation.2 | async-start | bytes 1310720 | tf_op jit(solution)/shard_map/all_gather | solution.py:62
  7.9 61.4 %all-gather.5.cloned.1.call-start = ((), (), s32[]{:S(2)}) async-start(), calls=%async_computation.3 | async-start | bytes 1310720 | tf_op jit(solution)/shard_map/all_gather | solution.py:63
  8.6 856.1 %all-reduce.3.cloned.1.call-start = ((), (), s32[]{:S(2)}) async-start(), calls=%async_computation.6 | async-start | bytes 67108864 | tf_op jit(solution)/shard_map/psum | solution.py:68
  9.4 2.7 copy-start.12
  10.8 73.3 %copy-start.1 = (pred[384]{0:T(512)(128)(4,1)}, pred[384]{0:T(512)(128)(4,1)S(1)}, u32[]{:S(2)}) copy-start(pred[384]{0:T(512)(128)(4,1)S(1)} %get-tuple-element.36) | copy-start | bytes 1156
  11.5 0.6 copy-start.14
  12.1 259.4 %copy-start.5 = (pred[384]{0:T(512)(128)(4,1)}, pred[384]{0:T(512)(128)(4,1)S(1)}, u32[]{:S(2)}) copy-start(pred[384]{0:T(512)(128)(4,1)S(1)} %get-tuple-element.34) | copy-start | bytes 1156
  301.6 7.9 copy-start.9
  454.4 0.7 copy-start.11
  454.4 749.3 %reduce-scatter.9.cloned.1.call-start = ((), (), s32[]{:S(2)}) async-start(), calls=%async_computation.5 | async-start | bytes 2621440
  897.6 15.4 %copy-start.3 = (pred[384]{0:T(512)(128)(4,1)S(1)}, pred[384]{0:T(512)(128)(4,1)}, u32[]{:S(2)}) copy-start(pred[384]{0:T(512)(128)(4,1)} %get-tuple-element.24) | copy-start | bytes 1156
  913.0 31.8 %copy-start.8 = (s32[384]{0:T(512)S(1)}, s32[384]{0:T(512)}, u32[]{:S(2)}) copy-start(s32[384]{0:T(512)} %get-tuple-element.39) | copy-start | bytes 4612
  944.8 76.4 %copy-start.10 = (s32[384]{0:T(512)S(1)}, s32[384]{0:T(512)}, u32[]{:S(2)}) copy-start(s32[384]{0:T(512)} %get-tuple-element.27) | copy-start | bytes 4612
  1021.1 182.7 %reduce-scatter.7.cloned.1.call-start = ((), (), s32[]{:S(2)}) async-start(), calls=%async_computation.4 | async-start | bytes 2621440
  1033.3 16.4 %copy-start = (pred[384]{0:T(512)(128)(4,1)S(1)}, pred[384]{0:T(512)(128)(4,1)}, u32[]{:S(2)}) copy-start(pred[384]{0:T(512)(128)(4,1)} %get-tuple-element.26) | copy-start | bytes 1156
  1049.7 30.3 %copy-start.7 = (s32[384]{0:T(512)S(1)}, s32[384]{0:T(512)}, u32[]{:S(2)}) copy-start(s32[384]{0:T(512)} %get-tuple-element.19) | copy-start | bytes 4612
  1080.0 76.8 %copy-start.2 = (pred[384]{0:T(512)(128)(4,1)S(1)}, pred[384]{0:T(512)(128)(4,1)}, u32[]{:S(2)}) copy-start(pred[384]{0:T(512)(128)(4,1)} %copy-done.1) | copy-start | bytes 1156
  1080.0 76.8 %copy-start.13 = (pred[384]{0:T(512)(128)(4,1)S(1)}, pred[384]{0:T(512)(128)(4,1)}, u32[]{:S(2)}) copy-start(pred[384]{0:T(512)(128)(4,1)} %copy-done.12) | copy-start | bytes 1156
  1156.9 23.2 %copy-start.4 = (pred[384]{0:T(512)(128)(4,1)S(1)}, pred[384]{0:T(512)(128)(4,1)}, u32[]{:S(2)}) copy-start(pred[384]{0:T(512)(128)(4,1)} %get-tuple-element.24) | copy-start | bytes 1156
  1156.9 23.2 %copy-start.6 = (pred[384]{0:T(512)(128)(4,1)S(1)}, pred[384]{0:T(512)(128)(4,1)}, u32[]{:S(2)}) copy-start(pred[384]{0:T(512)(128)(4,1)} %copy-done.5) | copy-start | bytes 1156
  1156.9 23.2 %copy-start.15 = (pred[384]{0:T(512)(128)(4,1)S(1)}, pred[384]{0:T(512)(128)(4,1)}, u32[]{:S(2)}) copy-start(pred[384]{0:T(512)(128)(4,1)} %copy-done.14) | copy-start | bytes 1156
Sparse Core Ops, SparseCore 0:
  9.6 30.6 all-gather.2
  41.8 27.4 all-gather.4
  454.5 410.1 all-reduce.2
  1021.2 44.5 reduce-scatter.8
  1157.0 43.9 reduce-scatter.6
where the time goes:
time: 1220 us; the launch traced here: 1210 us
  waiting for transfers between devices  465 us (38%)
  other arithmetic  391 us (32%)
  local copies, waits for them, and re-layouts  170 us (14%)
  matrix products  170 us (14%)
  between operations  14.5 us (1%)
    psum x1, waiting for transfers between devices, body(): pre_all = lax.psum(pre_terms, 'row')  410 us
    scatter-add x4, other arithmetic, sparse_apply(): jax.ops.segment_sum(products, targets, num_segments=segments + 1)[:segments]  365 us
    transpose x8, local copies, waits for them, and re-layouts, sparse_apply(): jnp.transpose(summed, (1, 0, 2))  64.8 us
    dot_general x2, matrix products, sparse_apply(): jnp.einsum('rsk,snk->srn', picked, blocks, preferred_element_type=jnp.flo...  63.2 us
    dot_general x2, matrix products, sparse_apply(): jnp.einsum('rsk,skn->srn', picked, blocks, preferred_element_type=jnp.flo...  60.1 us
    gather x4, local copies, waits for them, and re-layouts, sparse_apply(): picked = jnp.take(block_grid, source, axis=1)  56.5 us
    dot_general x2, matrix products, block_grads(): jnp.einsum('rsk,rsn->skn', picked_left, picked_right, preferred_element_t...  46.8 us
    all_gather x1, waiting for transfers between devices, body(): lax.all_gather(grad_out, 'col', axis=0, tiled=True)  26.9 us
  transfers between devices with their start and end apart: 5, of which 3 were waited for; matrix products, arithmetic and copies ran while one was open for 16% of the time, Pallas kernels for 0%

commit v1 on v0

v1 whole, which is shorter than its diff:
```python
import functools
import math

import jax
import jax.numpy as jnp
from jax import lax
from jax.experimental import pallas as pl
from jax.experimental.pallas import tpu as pltpu
from jax.sharding import PartitionSpec as P

FF = 65536
CHUNK = 32
VMEM_LIMIT = 58 * 1024 * 1024


def gelu_tanh(values):
    return jax.nn.gelu(values, approximate=True)


def contract(left, right, left_dim, right_dim):
    return lax.dot_general(
        left, right, (((left_dim,), (right_dim,)), ((), ())), preferred_element_type=jnp.float32
    )


def lanes(ref, index, width):
    return ref[:, pl.ds(pl.multiple_of(index * width, width), width)]


def to_hidden_kernel(flipped, source, target, panel, weights, keep, send, totals):
    step = pl.program_id(0)
    segments = totals.shape[0] - 1
    half = segments // 2
    width = weights.shape[-1]

    @pl.when(step == 0)
    def _():
        def clear(index, carry):
            totals[index] = jnp.zeros(totals.shape[1:], jnp.float32)
            return carry

        lax.fori_loop(0, segments, clear, 0)

    for slot in range(CHUNK):
        k = step * CHUNK + slot
        term = contract(
            lanes(panel, source[k], width), weights[slot], 1, 1 if flipped else 0
        )
        totals[target[k]] += term

    @pl.when(step == pl.num_programs(0) - 1)
    def _():
        def write(index, carry):
            keep[index] = totals[index]
            send[index] = totals[half + index].astype(jnp.bfloat16)
            return carry

        lax.fori_loop(0, half, write, 0)


def to_hidden(panel, weights, source, target, segments, flipped):
    tokens = panel.shape[0]
    slots, width, _ = weights.shape
    half = segments // 2
    return pl.pallas_call(
        functools.partial(to_hidden_kernel, flipped),
        grid_spec=pltpu.PrefetchScalarGridSpec(
            num_scalar_prefetch=2,
            grid=(slots // CHUNK,),
            in_specs=[
                pl.BlockSpec(panel.shape, lambda s, a, b: (0, 0)),
                pl.BlockSpec((CHUNK, width, width), lambda s, a, b: (s, 0, 0)),
            ],
            out_specs=[pl.BlockSpec((half, tokens, width), lambda s, a, b: (0, 0, 0))] * 2,
            scratch_shapes=[pltpu.VMEM((segments + 1, tokens, width), jnp.float32)],
        ),
        out_shape=[
            jax.ShapeDtypeStruct((half, tokens, width), jnp.float32),
            jax.ShapeDtypeStruct((half, tokens, width), jnp.bfloat16),
        ],
        compiler_params=pltpu.CompilerParams(vmem_limit_bytes=VMEM_LIMIT),
        cost_estimate=pl.CostEstimate(
            flops=8 * slots * tokens * width * width,
            bytes_accessed=2 * weights.size + 6 * half * tokens * width,
            transcendentals=0,
        ),
    )(source, target, panel, weights)


def to_model_kernel(transposed, pieces, model_at, hidden_at, live, panel, weights, *refs):
    hidden_parts = refs[:pieces]
    grads, own, send, totals, hidden, sems = refs[pieces:]
    step = pl.program_id(0)
    segments = totals.shape[0] - 1
    width = weights.shape[-1]
    share = own.shape[0]

    @pl.when(step == 0)
    def _():
        copies = []
        start = 0
        for number, part in enumerate(hidden_parts):
            count = part.shape[0]
            copies.append(
                pltpu.make_async_copy(part, hidden.at[pl.ds(start, count)], sems.at[number])
            )
            copies[-1].start()
            start += count
        totals[...] = jnp.zeros(totals.shape, jnp.float32)
        for copy in copies:
            copy.wait()

    for slot in range(CHUNK):
        k = step * CHUNK + slot
        model = model_at[k]
        values = hidden[hidden_at[k]]
        is_live = live[k] > 0
        term = contract(values, weights[slot], 1, 1 if transposed else 0)
        totals[jnp.where(is_live, model, segments)] += term
        other = lanes(panel, model, width)
        if transposed:
            grad = contract(other, values, 0, 0)
        else:
            grad = contract(values, other, 0, 0)
        grads[slot] = jnp.where(is_live, grad, 0.0).astype(jnp.bfloat16)

    @pl.when(step == pl.num_programs(0) - 1)
    def _():
        for segment in range(segments):
            columns = pl.ds(segment * width, width)
            own[:, columns] = totals[segment, pl.ds(0, share), :]
            for number in range(send.shape[0]):
                rows = pl.ds((number + 1) * share, share)
                send[number, :, columns] = totals[segment, rows, :].astype(jnp.bfloat16)


def to_model(panel, hidden_parts, weights, model_at, hidden_at, live, members, transposed):
    tokens, columns = panel.shape
    slots, width, _ = weights.shape
    segments = columns // width
    share = tokens // members
    hidden_count = sum(part.shape[0] for part in hidden_parts)
    pieces = len(hidden_parts)
    return pl.pallas_call(
        functools.partial(to_model_kernel, transposed, pieces),
        grid_spec=pltpu.PrefetchScalarGridSpec(
            num_scalar_prefetch=3,
            grid=(slots // CHUNK,),
            in_specs=[
                pl.BlockSpec(panel.shape, lambda s, a, b, c: (0, 0)),
                pl.BlockSpec((CHUNK, width, width), lambda s, a, b, c: (s, 0, 0)),
            ]
            + [pl.BlockSpec(memory_space=pl.ANY)] * pieces,
            out_specs=[
                pl.BlockSpec((CHUNK, width, width), lambda s, a, b, c: (s, 0, 0)),
                pl.BlockSpec((share, columns), lambda s, a, b, c: (0, 0)),
                pl.BlockSpec((members - 1, share, columns), lambda s, a, b, c: (0, 0, 0)),
            ],
            scratch_shapes=[
                pltpu.VMEM((segments + 1, tokens, width), jnp.float32),
                pltpu.VMEM((hidden_count, tokens, width), jnp.bfloat16),
                pltpu.SemaphoreType.DMA((pieces,)),
            ],
        ),
        out_shape=[
            jax.ShapeDtypeStruct(weights.shape, jnp.bfloat16),
            jax.ShapeDtypeStruct((share, columns), jnp.float32),
            jax.ShapeDtypeStruct((members - 1, share, columns), jnp.bfloat16),
        ],
        compiler_params=pltpu.CompilerParams(vmem_limit_bytes=VMEM_LIMIT),
        cost_estimate=pl.CostEstimate(
            flops=16 * slots * tokens * width * width,
            bytes_accessed=4 * weights.size + 2 * hidden_count * tokens * width,
            transcendentals=0,
        ),
    )(model_at, hidden_at, live, panel, weights, *hidden_parts)


def swap(values, bit):
    count = lax.axis_size("row")
    return lax.ppermute(values, "row", [(s, s ^ (1 << bit)) for s in range(count)])


def swap_orders():
    rest = list(range(1, int(math.log2(lax.axis_size("row")))))
    return [rest, rest[::-1]]


def hidden_position(index, segments):
    level = int(math.log2(segments))
    row = lax.axis_index("row")
    masks = []
    for order in swap_orders():
        mask = (row & 1) << (level - 1)
        for number, bit in enumerate(order):
            mask = mask | (((row >> bit) & 1) << (level - 3 - number))
        masks.append(mask)
    is_late = ((index >> (level - 2)) & 1) > 0
    return index ^ jnp.where(is_late, masks[1], masks[0])


def scatter_sum(keep, send):
    total = keep + swap(send, 0).astype(jnp.float32)
    quarter = total.shape[0] // 2
    parts = []
    for number, order in enumerate(swap_orders()):
        part = total[number * quarter : (number + 1) * quarter]
        for bit in order:
            half = part.shape[0] // 2
            arrived = swap(part[half:].astype(jnp.bfloat16), bit)
            part = part[:half] + arrived.astype(jnp.float32)
        parts.append(part)
    return parts


def gather_parts(parts):
    near, far = [], []
    for part, order in zip(parts, swap_orders()):
        stages = order[::-1]
        for bit in stages[:-1]:
            part = jnp.concatenate([part, swap(part, bit)], axis=0)
        pair = [part, swap(part, stages[-1])]
        near += pair
        far += [swap(piece, 0) for piece in pair]
    return near + far


def shift(values, distance):
    count = lax.axis_size("col")
    return lax.ppermute(values, "col", [(s, (s + distance) % count) for s in range(count)])


def gather_tokens(values):
    count = lax.axis_size("col")
    return jnp.concatenate([values] + [shift(values, -d) for d in range(1, count)], axis=0)


def scatter_tokens(own, send):
    total = own
    for number in range(send.shape[0]):
        total = total + shift(send[number], number + 1).astype(jnp.float32)
    return total


def body(activations, grad_out, first_blocks, first_coords, second_blocks, second_coords):
    width = first_blocks.shape[-1]
    members = lax.axis_size("col")
    row_tiles = activations.shape[1] // width
    col_tiles = FF // width // members
    row_base = lax.axis_index("row") * row_tiles
    col_base = lax.axis_index("col") * col_tiles

    def fields(model, hidden):
        is_live = model >= 0
        model_at = jnp.where(is_live, model - row_base, 0)
        hidden_at = jnp.where(is_live, hidden_position(hidden - col_base, col_tiles), 0)
        target = jnp.where(is_live, hidden_at, col_tiles)
        return model_at, hidden_at, target, is_live.astype(jnp.int32)

    model_one, hidden_one, target_one, live_one = fields(
        first_coords[0, 0, :, 0], first_coords[0, 0, :, 1]
    )
    model_two, hidden_two, target_two, live_two = fields(
        second_coords[0, 0, :, 1], second_coords[0, 0, :, 0]
    )
    weights_one = first_blocks[0, 0]
    weights_two = second_blocks[0, 0]

    inputs_all = gather_tokens(activations)
    cotangent_all = gather_tokens(grad_out)
    pre_parts = scatter_sum(
        *to_hidden(inputs_all, weights_one, model_one, target_one, col_tiles, False)
    )
    back_parts = scatter_sum(
        *to_hidden(cotangent_all, weights_two, model_two, target_two, col_tiles, True)
    )
    hidden_own, grad_pre_own = [], []
    for pre, back in zip(pre_parts, back_parts):
        hidden_full, gelu_back = jax.vjp(gelu_tanh, pre)
        hidden_own.append(hidden_full.astype(jnp.bfloat16))
        grad_pre_own.append(gelu_back(back)[0].astype(jnp.bfloat16))
    hidden_parts = gather_parts(hidden_own)
    grad_pre_parts = gather_parts(grad_pre_own)
    grad_second, own_out, send_out = to_model(
        cotangent_all, hidden_parts, weights_two, model_two, hidden_two, live_two, members, False
    )
    output = scatter_tokens(own_out, send_out)
    grad_first, own_in, send_in = to_model(
        inputs_all, grad_pre_parts, weights_one, model_one, hidden_one, live_one, members, True
    )
    grad_input = scatter_tokens(own_in, send_in)
    return (output, grad_input, grad_first[None, None], grad_second[None, None])


def solution(mesh):
    return jax.shard_map(
        body,
        mesh=mesh,
        in_specs=(
            P("col", "row"),
            P("col", "row"),
            P("row", "col", None, None, None),
            P("row", "col", None, None),
            P("col", "row", None, None, None),
            P("col", "row", None, None),
        ),
        out_specs=(
            P("col", "row"),
            P("col", "row"),
            P("row", "col", None, None, None),
            P("col", "row", None, None, None),
        ),
        check_vma=False,
    )
```

time: 1220 us -> 382 us (0.31)
  other arithmetic: 391 us -> 33.7 us
  waiting for transfers between devices: 465 us -> 179 us
  matrix products: 170 us -> 0 us
  local copies, waits for them, and re-layouts: 170 us -> 14.1 us
  Pallas kernels: 0 us -> 94.9 us
  starting transfers between devices: 0.2 us -> 57.2 us
  between operations: 14.5 us -> 0.95 us
    psum x1 -> x0, waiting for transfers between devices: 410 us -> none  [body(): pre_all = lax.psum(pre_terms, 'row')]
    scatter-add x4 -> x0, other arithmetic: 365 us -> none  [sparse_apply(): jax.ops.segment_sum(products, targets, num_segments=segments + 1)[:segments]]
    ppermute x0 -> x38, waiting for transfers between devices: none -> 179 us  [the longest x26 138 us: swap(): lax.ppermute(values, 'row', [(s, s ^ 1 << bit) for s in range(count)])]
    dot_general x6 -> x0, matrix products: 170 us -> none  [the longest x2 63.2 us: sparse_apply(): jnp.einsum('rsk,snk->srn', picked, blocks, preferred_element_type=jnp.flo...]
    pallas_call x0 -> x4, Pallas kernels: none -> 94.9 us  [the longest x2 50.5 us: to_model(): pl.pallas_call(functools.partial(to_model_kernel, transposed, pieces), gr...]
    transpose x8 -> x0, local copies, waits for them, and re-layouts: 64.8 us -> none  [sparse_apply(): jnp.transpose(summed, (1, 0, 2))]
    ppermute x0 -> x38, starting transfers between devices: none -> 57.2 us  [the longest x12 37.2 us: shift(): lax.ppermute(values, 'col', [(s, (s + distance) % count) for s in range(c...]
    gather x4 -> x0, local copies, waits for them, and re-layouts: 56.5 us -> none  [sparse_apply(): picked = jnp.take(block_grid, source, axis=1)]
  transfers between devices with their start and end apart: 5 -> 38, of which waited for: 3 -> 15; matrix products, arithmetic and copies ran while one was open for 16% -> 11% of each run, Pallas kernels for 0% -> 25%
where the time goes in v1:
time: 382 us; the launch traced here: 380 us
  waiting for transfers between devices  179 us (47%)
  Pallas kernels  94.9 us (25%)
  starting transfers between devices  57.2 us (15%)
  other arithmetic  33.7 us (9%)
  local copies, waits for them, and re-layouts  14.1 us (4%)
    ppermute x26, waiting for transfers between devices, swap(): lax.ppermute(values, 'row', [(s, s ^ 1 << bit) for s in range(count)])  138 us
    pallas_call x2, Pallas kernels, to_model(): pl.pallas_call(functools.partial(to_model_kernel, transposed, pieces), gr...  50.5 us
    pallas_call x2, Pallas kernels, to_hidden(): pl.pallas_call(functools.partial(to_hidden_kernel, flipped), grid_spec=pl...  44.4 us
    ppermute x12, waiting for transfers between devices, shift(): lax.ppermute(values, 'col', [(s, (s + distance) % count) for s in range(c...  41 us
    ppermute x12, starting transfers between devices, shift(): lax.ppermute(values, 'col', [(s, (s + distance) % count) for s in range(c...  37.2 us
    another operation x2, other arithmetic  20.2 us
    ppermute x26, starting transfers between devices, swap(): lax.ppermute(values, 'row', [(s, s ^ 1 << bit) for s in range(count)])  20 us
    unnamed x38, local copies, waits for them, and re-layouts  9.05 us
  transfers between devices with their start and end apart: 38, of which 15 were waited for; matrix products, arithmetic and copies ran while one was open for 11% of the time, Pallas kernels for 25%

profile of v1, /device:TPU:0, one launch (start us, length us, event | category | flops | bytes accessed | tf_op | source)
XLA Modules:
  0.0 380.3 jit_solution(12404551175968520453)
XLA Ops:
  0.6 4.1 %collective-permute-start.4 = (bf16[64,2048]{1,0:T(8,128)(2,1)}, bf16[64,2048]{1,0:T(8,128)(2,1)S(1)}, u32[]{:S(2)}, u32[]{:S(2)}) collective-permute-start(bf16[64,2048]{1,0:T(8,128)(2,1)} %param.6), channel_id=1, source_target_pairs={{0,2},{1,3},{2,0},{3,1},{4,6},{5,7},{6,4},{7,5},{8,10},{9,11},{10,... | collective-permute-start | bytes 786440 | tf_op jit(solution)/shard_map/ppermute | solution.py:230
  7.8 2.9 collective-permute-start
  16.7 16.5 %collective-permute-done = bf16[64,2048]{1,0:T(8,128)(2,1)S(1)} collective-permute-done((bf16[64,2048]{1,0:T(8,128)(2,1)}, bf16[64,2048]{1,0:T(8,128)(2,1)S(1)}, u32[]{:S(2)}, u32[]{:S(2)}) %collective-permute-start) | collective-permute-done | bytes 262176 | tf_op jit(solution)/shard_map/ppermute | solution.py:230
  33.2 18.0 %collective-permute-start.2 = (bf16[64,2048]{1,0:T(8,128)(2,1)}, bf16[64,2048]{1,0:T(8,128)(2,1)S(1)}, u32[]{:S(2)}, u32[]{:S(2)}) collective-permute-start(bf16[64,2048]{1,0:T(8,128)(2,1)} %param.7), channel_id=1, source_target_pairs={{0,1},{1,2},{2,3},{3,0},{4,5},{5,6},{6,7},{7,4},{8,9},{9,10},{10,1... | collective-permute-start | bytes 786440 | tf_op jit(solution)/shard_map/ppermute | solution.py:230
  52.6 3.9 %collective-permute-done.2 = bf16[64,2048]{1,0:T(8,128)(2,1)S(1)} collective-permute-done((bf16[64,2048]{1,0:T(8,128)(2,1)}, bf16[64,2048]{1,0:T(8,128)(2,1)S(1)}, u32[]{:S(2)}, u32[]{:S(2)}) %collective-permute-start.2) | collective-permute-done | bytes 262176 | tf_op jit(solution)/shard_map/ppermute | solution.py:230
  57.2 22.1 %shard_map.95 = (f32[64,256,128]{2,1,0:T(8,128)}, bf16[64,256,128]{2,1,0:T(8,128)(2,1)}) custom-call(s32[384]{0:T(512)} %get-tuple-element.55.model_at.source, s32[384]{0:T(512)} %get-tuple-element.30.target, bf16[256,2048]{1,0:T(8,128)(2,1)} %constant_dynamic-update-slice_fusion.panel, bf16[384,128,128]{2,1,0:T(8,128)(2,1)} %bitcast.20), custom_call_target="tpu_custom_call" | custom-call | flops 12884901888 | bytes 25165824 | tf_op jit(solution)/shard_map/pallas_call | solution.py:65
  80.5 22.2 %shard_map.93 = (f32[64,256,128]{2,1,0:T(8,128)}, bf16[64,256,128]{2,1,0:T(8,128)(2,1)}) custom-call(s32[384]{0:T(512)} %get-tuple-element.54.source.model_at, s32[384]{0:T(512)} %get-tuple-element.34.target, bf16[256,2048]{1,0:T(8,128)(2,1)} %copy-done.6, bf16[384,128,128]{2,1,0:T(8,128)(2,1)} %bitcast.18), custom_call_target="tpu_custom_call" | custom-call | flops 12884901888 | bytes 25165824 | tf_op jit(solution)/shard_map/pallas_call | solution.py:65
  105.3 10.1 %fusion.14 = (bf16[64,256,128]{2,1,0:T(8,128)(2,1)S(1)}, f32[64,256,128]{2,1,0:T(8,128)}) fusion(f32[64,256,128]{2,1,0:T(8,128)} %get-tuple-element.18, bf16[64,256,128]{2,1,0:T(8,128)(2,1)} %copy-done), kind=kLoop, calls=%fused_computation.68 | loop fusion | flops 6291456 | bytes 25165824 | tf_op jit(solution)/shard_map/convert.3
  119.6 10.1 %fusion.15 = (bf16[64,256,128]{2,1,0:T(8,128)(2,1)S(1)}, f32[64,256,128]{2,1,0:T(8,128)}) fusion(f32[64,256,128]{2,1,0:T(8,128)} %get-tuple-element.14, bf16[64,256,128]{2,1,0:T(8,128)(2,1)} %collective-permute-done.6), kind=kLoop, calls=%fused_computation.69 | loop fusion | flops 6291456 | bytes 25165824 | tf_op jit(solution)/shard_map/convert.7
  131.3 11.8 %collective-permute-done.27 = bf16[16,256,128]{2,1,0:T(8,128)(2,1)S(1)} collective-permute-done((bf16[16,256,128]{2,1,0:T(8,128)(2,1)}, bf16[16,256,128]{2,1,0:T(8,128)(2,1)S(1)}, u32[]{:S(2)}, u32[]{:S(2)}) %collective-permute-start.27) | collective-permute-done | bytes 1048608 | tf_op jit(solution)/shard_map/ppermute | solution.py:181
  144.4 3.0 slice_add_fusion
  149.0 15.6 %collective-permute-done.11 = bf16[16,256,128]{2,1,0:T(8,128)(2,1)S(1)} collective-permute-done((bf16[16,256,128]{2,1,0:T(8,128)(2,1)S(1)}, bf16[16,256,128]{2,1,0:T(8,128)(2,1)S(1)}, u32[]{:S(2)}, u32[]{:S(2)}) %collective-permute-start.11) | collective-permute-done | bytes 1048608 | tf_op jit(solution)/shard_map/ppermute | solution.py:181
  171.5 6.6 %collective-permute-done.28 = bf16[8,256,128]{2,1,0:T(8,128)(2,1)S(1)} collective-permute-done((bf16[8,256,128]{2,1,0:T(8,128)(2,1)S(1)}, bf16[8,256,128]{2,1,0:T(8,128)(2,1)S(1)}, u32[]{:S(2)}, u32[]{:S(2)}) %collective-permute-start.28) | collective-permute-done | bytes 524320 | tf_op jit(solution)/shard_map/ppermute | solution.py:181
  178.1 10.0 %collective-permute-done.12 = bf16[8,256,128]{2,1,0:T(8,128)(2,1)S(1)} collective-permute-done((bf16[8,256,128]{2,1,0:T(8,128)(2,1)S(1)}, bf16[8,256,128]{2,1,0:T(8,128)(2,1)S(1)}, u32[]{:S(2)}, u32[]{:S(2)}) %collective-permute-start.12) | collective-permute-done | bytes 524320 | tf_op jit(solution)/shard_map/ppermute | solution.py:181
  193.3 19.7 %collective-permute-done.13 = bf16[8,256,128]{2,1,0:T(8,128)(2,1)S(1)} collective-permute-done((bf16[8,256,128]{2,1,0:T(8,128)(2,1)S(1)}, bf16[8,256,128]{2,1,0:T(8,128)(2,1)S(1)}, u32[]{:S(2)}, u32[]{:S(2)}) %collective-permute-start.13) | collective-permute-done | bytes 524320 | tf_op jit(solution)/shard_map/ppermute | solution.py:181
  217.5 52.3 %collective-permute-done.9 = bf16[8,256,128]{2,1,0:T(8,128)(2,1)S(1)} collective-permute-done((bf16[8,256,128]{2,1,0:T(8,128)(2,1)S(1)}, bf16[8,256,128]{2,1,0:T(8,128)(2,1)S(1)}, u32[]{:S(2)}, u32[]{:S(2)}) %collective-permute-start.9) | collective-permute-done | bytes 524320 | tf_op jit(solution)/shard_map/ppermute | solution.py:181
  273.8 18.4 %collective-permute-done.10.refs_1_ = bf16[16,256,128]{2,1,0:T(8,128)(2,1)} collective-permute-done((bf16[16,256,128]{2,1,0:T(8,128)(2,1)S(1)}, bf16[16,256,128]{2,1,0:T(8,128)(2,1)}, u32[]{:S(2)}, u32[]{:S(2)}) %collective-permute-start.10) | collective-permute-done | bytes 1048608 | tf_op jit(solution)/shard_map/ppermute | solution.py:181
  294.7 25.5 %shard_map.96 = (bf16[384,128,128]{2,1,0:T(8,128)(2,1)}, f32[64,2048]{1,0:T(8,128)}, bf16[3,64,2048]{2,1,0:T(8,128)(2,1)}) custom-call(s32[384]{0:T(512)} %get-tuple-element.54.source.model_at, s32[384]{0:T(512)} %get-tuple-element.35.hidden_at, s32[384]{0:T(512)} %convert_element_type.85.live, bf16[256,2048]{1,0:T(8,128)(2,1)} %copy-done.6, ...), custom_call_target="tpu_custom_call" | custom-call | flops 25769803776 | bytes 33554432 | tf_op jit(solution)/shard_map/pallas_call | solution.py:144
  321.5 2.4 collective-permute-start.35
  325.8 25.0 %shard_map.94 = (bf16[384,128,128]{2,1,0:T(8,128)(2,1)}, f32[64,2048]{1,0:T(8,128)}, bf16[3,64,2048]{2,1,0:T(8,128)(2,1)}) custom-call(s32[384]{0:T(512)} %get-tuple-element.55.model_at.source, s32[384]{0:T(512)} %get-tuple-element.31.hidden_at, s32[384]{0:T(512)} %convert_element_type.74.live, bf16[256,2048]{1,0:T(8,128)(2,1)} %constant_dynamic-update-slice_fusion.panel, ...), custom_call_target="tpu_custom_call" | custom-call | flops 25769803776 | bytes 33554432 | tf_op jit(solution)/shard_map/pallas_call | solution.py:144
  352.3 3.6 collective-permute-start.21
  357.8 5.4 %collective-permute-done.19 = bf16[64,2048]{1,0:T(8,128)(2,1)S(1)} collective-permute-done((bf16[64,2048]{1,0:T(8,128)(2,1)S(1)}, bf16[64,2048]{1,0:T(8,128)(2,1)S(1)}, u32[]{:S(2)}, u32[]{:S(2)}) %collective-permute-start.19) | collective-permute-done | bytes 262176 | tf_op jit(solution)/shard_map/ppermute | solution.py:230
  363.2 3.4 collective-permute-done.21
  366.6 11.8 %collective-permute-done.20 = bf16[64,2048]{1,0:T(8,128)(2,1)S(1)} collective-permute-done((bf16[64,2048]{1,0:T(8,128)(2,1)S(1)}, bf16[64,2048]{1,0:T(8,128)(2,1)S(1)}, u32[]{:S(2)}, u32[]{:S(2)}) %collective-permute-start.20) | collective-permute-done | bytes 262176 | tf_op jit(solution)/shard_map/ppermute | solution.py:230
  (124 shorter events, 55.1 us)
Async XLA Ops:
  0.6 78.8 %collective-permute-start.4 = (bf16[64,2048]{1,0:T(8,128)(2,1)}, bf16[64,2048]{1,0:T(8,128)(2,1)S(1)}, u32[]{:S(2)}, u32[]{:S(2)}) collective-permute-start(bf16[64,2048]{1,0:T(8,128)(2,1)} %param.6), channel_id=1, source_target_pairs={{0,2},{1,3},{2,0},{3,1},{4,6},{5,7},{6,4},{7,5},{8,10},{9,11},{10,... | collective-permute-start | bytes 786440 | tf_op jit(solution)/shard_map/ppermute | solution.py:230
  4.7 74.6 %collective-permute-start.3 = (bf16[64,2048]{1,0:T(8,128)(2,1)}, bf16[64,2048]{1,0:T(8,128)(2,1)S(1)}, u32[]{:S(2)}, u32[]{:S(2)}) collective-permute-start(bf16[64,2048]{1,0:T(8,128)(2,1)} %param.6), channel_id=1, source_target_pairs={{0,3},{1,0},{2,1},{3,2},{4,7},{5,4},{6,5},{7,6},{8,11},{9,8},{10,9... | collective-permute-start | bytes 786440 | tf_op jit(solution)/shard_map/ppermute | solution.py:230
  6.1 73.4 %collective-permute-start.5 = (bf16[64,2048]{1,0:T(8,128)(2,1)}, bf16[64,2048]{1,0:T(8,128)(2,1)S(1)}, u32[]{:S(2)}, u32[]{:S(2)}) collective-permute-start(bf16[64,2048]{1,0:T(8,128)(2,1)} %param.6), channel_id=1, source_target_pairs={{0,1},{1,2},{2,3},{3,0},{4,5},{5,6},{6,7},{7,4},{8,9},{9,10},{10,1... | collective-permute-start | bytes 786440 | tf_op jit(solution)/shard_map/ppermute | solution.py:230
  6.8 45.1 %collective-permute-start.1 = (bf16[64,2048]{1,0:T(8,128)(2,1)}, bf16[64,2048]{1,0:T(8,128)(2,1)S(1)}, u32[]{:S(2)}, u32[]{:S(2)}) collective-permute-start(bf16[64,2048]{1,0:T(8,128)(2,1)} %param.7), channel_id=1, source_target_pairs={{0,2},{1,3},{2,0},{3,1},{4,6},{5,7},{6,4},{7,5},{8,10},{9,11},{10,... | collective-permute-start | bytes 786440 | tf_op jit(solution)/shard_map/ppermute | solution.py:230
  7.8 25.4 %collective-permute-start = (bf16[64,2048]{1,0:T(8,128)(2,1)}, bf16[64,2048]{1,0:T(8,128)(2,1)S(1)}, u32[]{:S(2)}, u32[]{:S(2)}) collective-permute-start(bf16[64,2048]{1,0:T(8,128)(2,1)} %param.7), channel_id=1, source_target_pairs={{0,3},{1,0},{2,1},{3,2},{4,7},{5,4},{6,5},{7,6},{8,11},{9,8},{10,9... | collective-permute-start | bytes 786440 | tf_op jit(solution)/shard_map/ppermute | solution.py:230
  79.4 23.8 %collective-permute-start.22 = (bf16[64,256,128]{2,1,0:T(8,128)(2,1)}, bf16[64,256,128]{2,1,0:T(8,128)(2,1)S(1)}, u32[]{:S(2)}, u32[]{:S(2)}) collective-permute-start(bf16[64,256,128]{2,1,0:T(8,128)(2,1)} %get-tuple-element.19), channel_id=1, source_target_pairs={{0,4},{4,0},{8,12},{12,8},{16,20},{20,16},{24,28},{28,24},{1,5},{5... | collective-permute-start | bytes 12582920 | tf_op jit(solution)/shard_map/ppermute | solution.py:181
  116.8 26.2 %collective-permute-start.27 = (bf16[16,256,128]{2,1,0:T(8,128)(2,1)}, bf16[16,256,128]{2,1,0:T(8,128)(2,1)S(1)}, u32[]{:S(2)}, u32[]{:S(2)}) collective-permute-start(bf16[16,256,128]{2,1,0:T(8,128)(2,1)} %get-tuple-element.40), channel_id=1, source_target_pairs={{0,16},{4,20},{8,24},{12,28},{16,0},{20,4},{24,8},{28,12},{1,17},{... | collective-permute-start | bytes 3145736 | tf_op jit(solution)/shard_map/ppermute | solution.py:181
  118.1 26.3 %collective-permute-start.23 = (bf16[16,256,128]{2,1,0:T(8,128)(2,1)}, bf16[16,256,128]{2,1,0:T(8,128)(2,1)S(1)}, u32[]{:S(2)}, u32[]{:S(2)}) collective-permute-start(bf16[16,256,128]{2,1,0:T(8,128)(2,1)} %get-tuple-element.41), channel_id=1, source_target_pairs={{0,8},{4,12},{8,0},{12,4},{16,24},{20,28},{24,16},{28,20},{1,9},{5... | collective-permute-start | bytes 3145736 | tf_op jit(solution)/shard_map/ppermute | solution.py:181
  129.9 34.7 %collective-permute-start.11 = (bf16[16,256,128]{2,1,0:T(8,128)(2,1)S(1)}, bf16[16,256,128]{2,1,0:T(8,128)(2,1)S(1)}, u32[]{:S(2)}, u32[]{:S(2)}) collective-permute-start(bf16[16,256,128]{2,1,0:T(8,128)(2,1)S(1)} %get-tuple-element.42), channel_id=1, source_target_pairs={{0,16},{4,20},{8,24},{12,28},{16,0},{20,4},{24,8},{28,12},{1,17},{... | collective-permute-start | bytes 3145736 | tf_op jit(solution)/shard_map/ppermute | solution.py:181
  130.5 36.4 %collective-permute-start.7 = (bf16[16,256,128]{2,1,0:T(8,128)(2,1)S(1)}, bf16[16,256,128]{2,1,0:T(8,128)(2,1)S(1)}, u32[]{:S(2)}, u32[]{:S(2)}) collective-permute-start(bf16[16,256,128]{2,1,0:T(8,128)(2,1)S(1)} %get-tuple-element.43), channel_id=1, source_target_pairs={{0,8},{4,12},{8,0},{12,4},{16,24},{20,28},{24,16},{28,20},{1,9},{5... | collective-permute-start | bytes 3145736 | tf_op jit(solution)/shard_map/ppermute | solution.py:181
  147.4 30.7 %collective-permute-start.28 = (bf16[8,256,128]{2,1,0:T(8,128)(2,1)S(1)}, bf16[8,256,128]{2,1,0:T(8,128)(2,1)S(1)}, u32[]{:S(2)}, u32[]{:S(2)}) collective-permute-start(bf16[8,256,128]{2,1,0:T(8,128)(2,1)S(1)} %slice.176), channel_id=1, source_target_pairs={{0,8},{4,12},{8,0},{12,4},{16,24},{20,28},{24,16},{28,20},{1,9},{5... | collective-permute-start | bytes 1572872 | tf_op jit(solution)/shard_map/ppermute | solution.py:181
  189.0 24.9 %collective-permute-start.29 = (bf16[8,256,128]{2,1,0:T(8,128)(2,1)S(1)}, bf16[8,256,128]{2,1,0:T(8,128)(2,1)S(1)}, u32[]{:S(2)}, u32[]{:S(2)}) collective-permute-start(bf16[8,256,128]{2,1,0:T(8,128)(2,1)S(1)} %get-tuple-element.44), channel_id=1, source_target_pairs={{0,8},{4,12},{8,0},{12,4},{16,24},{20,28},{24,16},{28,20},{1,9},{5... | collective-permute-start | bytes 1572872 | tf_op jit(solution)/shard_map/ppermute | solution.py:181
  213.1 58.4 %collective-permute-start.14 = (bf16[16,256,128]{2,1,0:T(8,128)(2,1)S(1)}, bf16[16,256,128]{2,1,0:T(8,128)(2,1)S(1)}, u32[]{:S(2)}, u32[]{:S(2)}) collective-permute-start(bf16[16,256,128]{2,1,0:T(8,128)(2,1)S(1)} %pad_maximum_fusion.1.refs_2_), channel_id=1, source_target_pairs={{0,16},{4,20},{8,24},{12,28},{16,0},{20,4},{24,8},{28,12},{1,17},{... | collective-permute-start | bytes 3145736 | tf_op jit(solution)/shard_map/ppermute | solution.py:181
  214.0 57.5 %collective-permute-start.30 = (bf16[16,256,128]{2,1,0:T(8,128)(2,1)S(1)}, bf16[16,256,128]{2,1,0:T(8,128)(2,1)S(1)}, u32[]{:S(2)}, u32[]{:S(2)}) collective-permute-start(bf16[16,256,128]{2,1,0:T(8,128)(2,1)S(1)} %pad_maximum_fusion.3.refs_2_), channel_id=1, source_target_pairs={{0,16},{4,20},{8,24},{12,28},{16,0},{20,4},{24,8},{28,12},{1,17},{... | collective-permute-start | bytes 3145736 | tf_op jit(solution)/shard_map/ppermute | solution.py:181
  215.4 56.5 %collective-permute-start.26 = (bf16[16,256,128]{2,1,0:T(8,128)(2,1)S(1)}, bf16[16,256,128]{2,1,0:T(8,128)(2,1)S(1)}, u32[]{:S(2)}, u32[]{:S(2)}) collective-permute-start(bf16[16,256,128]{2,1,0:T(8,128)(2,1)S(1)} %pad_maximum_fusion.2.refs_0_), channel_id=1, source_target_pairs={{0,8},{4,12},{8,0},{12,4},{16,24},{20,28},{24,16},{28,20},{1,9},{5... | collective-permute-start | bytes 3145736 | tf_op jit(solution)/shard_map/ppermute | solution.py:181
  217.0 52.8 %collective-permute-start.9 = (bf16[8,256,128]{2,1,0:T(8,128)(2,1)S(1)}, bf16[8,256,128]{2,1,0:T(8,128)(2,1)S(1)}, u32[]{:S(2)}, u32[]{:S(2)}) collective-permute-start(bf16[8,256,128]{2,1,0:T(8,128)(2,1)S(1)} %get-tuple-element.47), channel_id=1, source_target_pairs={{0,16},{4,20},{8,24},{12,28},{16,0},{20,4},{24,8},{28,12},{1,17},{... | collective-permute-start | bytes 1572872 | tf_op jit(solution)/shard_map/ppermute | solution.py:181
  217.5 55.9 %collective-permute-start.33 = (bf16[16,256,128]{2,1,0:T(8,128)(2,1)S(1)}, bf16[16,256,128]{2,1,0:T(8,128)(2,1)S(1)}, u32[]{:S(2)}, u32[]{:S(2)}) collective-permute-start(bf16[16,256,128]{2,1,0:T(8,128)(2,1)S(1)} %pad_maximum_fusion.3.refs_2_), channel_id=1, source_target_pairs={{0,4},{4,0},{8,12},{12,8},{16,20},{20,16},{24,28},{28,24},{1,5},{5... | collective-permute-start | bytes 3145736 | tf_op jit(solution)/shard_map/ppermute | solution.py:181
  273.4 50.4 %collective-permute-start.17 = (bf16[16,256,128]{2,1,0:T(8,128)(2,1)S(1)}, bf16[16,256,128]{2,1,0:T(8,128)(2,1)}, u32[]{:S(2)}, u32[]{:S(2)}) collective-permute-start(bf16[16,256,128]{2,1,0:T(8,128)(2,1)S(1)} %pad_maximum_fusion.1.refs_2_), channel_id=1, source_target_pairs={{0,4},{4,0},{8,12},{12,8},{16,20},{20,16},{24,28},{28,24},{1,5},{5... | collective-permute-start | bytes 3145736 | tf_op jit(solution)/shard_map/ppermute | solution.py:181
  292.2 33.2 %collective-permute-start.15 = (bf16[16,256,128]{2,1,0:T(8,128)(2,1)S(1)}, bf16[16,256,128]{2,1,0:T(8,128)(2,1)}, u32[]{:S(2)}, u32[]{:S(2)}) collective-permute-start(bf16[16,256,128]{2,1,0:T(8,128)(2,1)S(1)} %pad_maximum_fusion.refs_0_), channel_id=1, source_target_pairs={{0,4},{4,0},{8,12},{12,8},{16,20},{20,16},{24,28},{28,24},{1,5},{5... | collective-permute-start | bytes 3145736 | tf_op jit(solution)/shard_map/ppermute | solution.py:181
  292.2 33.6 %collective-permute-start.18 = (bf16[16,256,128]{2,1,0:T(8,128)(2,1)S(1)}, bf16[16,256,128]{2,1,0:T(8,128)(2,1)}, u32[]{:S(2)}, u32[]{:S(2)}) collective-permute-start(bf16[16,256,128]{2,1,0:T(8,128)(2,1)S(1)} %collective-permute-done.14.refs_3_), channel_id=1, source_target_pairs={{0,4},{4,0},{8,12},{12,8},{16,20},{20,16},{24,28},{28,24},{1,5},{5... | collective-permute-start | bytes 3145736 | tf_op jit(solution)/shard_map/ppermute | solution.py:181
  292.8 33.0 %collective-permute-start.16 = (bf16[16,256,128]{2,1,0:T(8,128)(2,1)}, bf16[16,256,128]{2,1,0:T(8,128)(2,1)}, u32[]{:S(2)}, u32[]{:S(2)}) collective-permute-start(bf16[16,256,128]{2,1,0:T(8,128)(2,1)} %collective-permute-done.10.refs_1_), channel_id=1, source_target_pairs={{0,4},{4,0},{8,12},{12,8},{16,20},{20,16},{24,28},{28,24},{1,5},{5... | collective-permute-start | bytes 3145736 | tf_op jit(solution)/shard_map/ppermute | solution.py:181
  321.5 34.4 %collective-permute-start.35 = (bf16[64,2048]{1,0:T(8,128)(2,1)S(1)}, bf16[64,2048]{1,0:T(8,128)(2,1)S(1)}, u32[]{:S(2)}, u32[]{:S(2)}) collective-permute-start(bf16[64,2048]{1,0:T(8,128)(2,1)S(1)} %get-tuple-element.48), channel_id=1, source_target_pairs={{0,1},{1,2},{2,3},{3,0},{4,5},{5,6},{6,7},{7,4},{8,9},{9,10},{10,1... | collective-permute-start | bytes 786440 | tf_op jit(solution)/shard_map/ppermute | solution.py:230
  323.8 33.0 %collective-permute-start.37 = (bf16[64,2048]{1,0:T(8,128)(2,1)S(1)}, bf16[64,2048]{1,0:T(8,128)(2,1)S(1)}, u32[]{:S(2)}, u32[]{:S(2)}) collective-permute-start(bf16[64,2048]{1,0:T(8,128)(2,1)S(1)} %get-tuple-element.49), channel_id=1, source_target_pairs={{0,3},{1,0},{2,1},{3,2},{4,7},{5,4},{6,5},{7,6},{8,11},{9,8},{10,9... | collective-permute-start | bytes 786440 | tf_op jit(solution)/shard_map/ppermute | solution.py:230
  325.3 31.5 %collective-permute-start.36 = (bf16[64,2048]{1,0:T(8,128)(2,1)S(1)}, bf16[64,2048]{1,0:T(8,128)(2,1)S(1)}, u32[]{:S(2)}, u32[]{:S(2)}) collective-permute-start(bf16[64,2048]{1,0:T(8,128)(2,1)S(1)} %get-tuple-element.50), channel_id=1, source_target_pairs={{0,2},{1,3},{2,0},{3,1},{4,6},{5,7},{6,4},{7,5},{8,10},{9,11},{10,... | collective-permute-start | bytes 786440 | tf_op jit(solution)/shard_map/ppermute | solution.py:230
  (30 other events, 806.2 us)

commit v2 on v1

--- a/solution.py
+++ b/solution.py
@@ -87,93 +87,120 @@
     )(source, target, panel, weights)
 
 
-def to_model_kernel(transposed, pieces, model_at, hidden_at, live, panel, weights, *refs):
-    hidden_parts = refs[:pieces]
-    grads, own, send, totals, hidden, sems = refs[pieces:]
+def fetch(parts, hidden, sems):
+    copies = []
+    start = 0
+    for number, part in enumerate(parts):
+        count = part.shape[0]
+        copies.append(pltpu.make_async_copy(part, hidden.at[pl.ds(start, count)], sems.at[number]))
+        copies[-1].start()
+        start += count
+    for copy in copies:
+        copy.wait()
+
+
+def to_model_kernel(transposed, pieces, with_sums, with_grads, model_at, hidden_at, live, *refs):
+    refs = list(refs)
+    panel = refs.pop(0) if with_grads else None
+    weights = refs.pop(0) if with_sums else None
+    hidden_parts = [refs.pop(0) for _ in range(pieces)]
+    grads = refs.pop(0) if with_grads else None
+    own, send, totals = [refs.pop(0) for _ in range(3)] if with_sums else (None, None, None)
+    hidden, sems = refs
     step = pl.program_id(0)
-    segments = totals.shape[0] - 1
-    width = weights.shape[-1]
-    share = own.shape[0]
+    width = hidden.shape[-1]
 
     @pl.when(step == 0)
     def _():
-        copies = []
-        start = 0
-        for number, part in enumerate(hidden_parts):
-            count = part.shape[0]
-            copies.append(
-                pltpu.make_async_copy(part, hidden.at[pl.ds(start, count)], sems.at[number])
-            )
-            copies[-1].start()
-            start += count
-        totals[...] = jnp.zeros(totals.shape, jnp.float32)
-        for copy in copies:
-            copy.wait()
+        if with_sums:
+            totals[...] = jnp.zeros(totals.shape, jnp.float32)
+        fetch(hidden_parts, hidden, sems)
 
     for slot in range(CHUNK):
         k = step * CHUNK + slot
         model = model_at[k]
         values = hidden[hidden_at[k]]
         is_live = live[k] > 0
-        term = contract(values, weights[slot], 1, 1 if transposed else 0)
-        totals[jnp.where(is_live, model, segments)] += term
-        other = lanes(panel, model, width)
-        if transposed:
-            grad = contract(other, values, 0, 0)
-        else:
-            grad = contract(values, other, 0, 0)
-        grads[slot] = jnp.where(is_live, grad, 0.0).astype(jnp.bfloat16)
-
-    @pl.when(step == pl.num_programs(0) - 1)
-    def _():
-        for segment in range(segments):
-            columns = pl.ds(segment * width, width)
-            own[:, columns] = totals[segment, pl.ds(0, share), :]
-            for number in range(send.shape[0]):
-                rows = pl.ds((number + 1) * share, share)
-                send[number, :, columns] = totals[segment, rows, :].astype(jnp.bfloat16)
-
-
-def to_model(panel, hidden_parts, weights, model_at, hidden_at, live, members, transposed):
+        if with_sums:
+            term = contract(values, weights[slot], 1, 1 if transposed else 0)
+            totals[jnp.where(is_live, model, totals.shape[0] - 1)] += term
+        if with_grads:
+            other = lanes(panel, model, width)
+            if transposed:
+                grad = contract(other, values, 0, 0)
+            else:
+                grad = contract(values, other, 0, 0)
+            grads[slot] = jnp.where(is_live, grad, 0.0).astype(jnp.bfloat16)
+
+    if with_sums:
+
+        @pl.when(step == pl.num_programs(0) - 1)
+        def _():
+            share = own.shape[0]
+            for segment in range(totals.shape[0] - 1):
+                columns = pl.ds(segment * width, width)
+                own[:, columns] = totals[segment, pl.ds(0, share), :]
+                for number, piece in enumerate(send):
+                    rows = pl.ds((number + 1) * share, share)
+                    piece[:, columns] = totals[segment, rows, :].astype(jnp.bfloat16)
+
+
+def to_model(
+    panel, hidden_parts, weights, places, members, transposed, with_sums=True, with_grads=True
+):
     tokens, columns = panel.shape
     slots, width, _ = weights.shape
     segments = columns // width
     share = tokens // members
     hidden_count = sum(part.shape[0] for part in hidden_parts)
     pieces = len(hidden_parts)
+    chunk_spec = pl.BlockSpec((CHUNK, width, width), lambda s, a, b, c: (s, 0, 0))
+    share_spec = pl.BlockSpec((share, columns), lambda s, a, b, c: (0, 0))
+    operands, in_specs, out_specs, out_shape, scratch = [], [], [], [], []
+    if with_grads:
+        operands.append(panel)
+        in_specs.append(pl.BlockSpec(panel.shape, lambda s, a, b, c: (0, 0)))
+        out_specs.append(chunk_spec)
+        out_shape.append(jax.ShapeDtypeStruct(weights.shape, jnp.bfloat16))
+    if with_sums:
+        operands.append(weights)
+        in_specs.append(chunk_spec)
+        out_specs += [share_spec, [share_spec] * (members - 1)]
+        out_shape += [
+            jax.ShapeDtypeStruct((share, columns), jnp.float32),
+            [jax.ShapeDtypeStruct((share, columns), jnp.bfloat16)] * (members - 1),
+        ]
+        scratch.append(pltpu.VMEM((segments + 1, tokens, width), jnp.float32))
+    scratch += [
+        pltpu.VMEM((hidden_count, tokens, width), jnp.bfloat16),
+        pltpu.SemaphoreType.DMA((pieces,)),
+    ]
+
+    def kernel(*refs):
+        flat = list(refs)
+        if with_sums:
+            start = 3 + len(operands) + pieces + (1 if with_grads else 0) + 1
+            if not isinstance(flat[start], (list, tuple)):
+                flat[start : start + members - 1] = [flat[start : start + members - 1]]
+        to_model_kernel(transposed, pieces, with_sums, with_grads, *flat)
+
     return pl.pallas_call(
-        functools.partial(to_model_kernel, transposed, pieces),
+        kernel,
         grid_spec=pltpu.PrefetchScalarGridSpec(
             num_scalar_prefetch=3,
             grid=(slots // CHUNK,),
-            in_specs=[
-                pl.BlockSpec(panel.shape, lambda s, a, b, c: (0, 0)),
-                pl.BlockSpec((CHUNK, width, width), lambda s, a, b, c: (s, 0, 0)),
-            ]
-            + [pl.BlockSpec(memory_space=pl.ANY)] * pieces,
-            out_specs=[
-                pl.BlockSpec((CHUNK, width, width), lambda s, a, b, c: (s, 0, 0)),
-                pl.BlockSpec((share, columns), lambda s, a, b, c: (0, 0)),
-                pl.BlockSpec((members - 1, share, columns), lambda s, a, b, c: (0, 0, 0)),
-            ],
-            scratch_shapes=[
-                pltpu.VMEM((segments + 1, tokens, width), jnp.float32),
-                pltpu.VMEM((hidden_count, tokens, width), jnp.bfloat16),
-                pltpu.SemaphoreType.DMA((pieces,)),
-            ],
-        ),
-        out_shape=[
-            jax.ShapeDtypeStruct(weights.shape, jnp.bfloat16),
-            jax.ShapeDtypeStruct((share, columns), jnp.float32),
-            jax.ShapeDtypeStruct((members - 1, share, columns), jnp.bfloat16),
-        ],
+            in_specs=in_specs + [pl.BlockSpec(memory_space=pl.ANY)] * pieces,
+            out_specs=out_specs,
+            scratch_shapes=scratch,
+        ),
+        out_shape=out_shape,
         compiler_params=pltpu.CompilerParams(vmem_limit_bytes=VMEM_LIMIT),
         cost_estimate=pl.CostEstimate(
-            flops=16 * slots * tokens * width * width,
+            flops=8 * slots * tokens * width * width * (with_sums + with_grads),
             bytes_accessed=4 * weights.size + 2 * hidden_count * tokens * width,
             transcendentals=0,
         ),
-    )(model_at, hidden_at, live, panel, weights, *hidden_parts)
+    )(*places, *operands, *hidden_parts)
 
 
 def swap(values, bit):
@@ -199,30 +226,55 @@
     return index ^ jnp.where(is_late, masks[1], masks[0])
 
 
-def scatter_sum(keep, send):
-    total = keep + swap(send, 0).astype(jnp.float32)
-    quarter = total.shape[0] // 2
-    parts = []
-    for number, order in enumerate(swap_orders()):
-        part = total[number * quarter : (number + 1) * quarter]
-        for bit in order:
-            half = part.shape[0] // 2
-            arrived = swap(part[half:].astype(jnp.bfloat16), bit)
-            part = part[:half] + arrived.astype(jnp.float32)
-        parts.append(part)
-    return parts
-
-
-def gather_parts(parts):
-    near, far = [], []
+def after(values, *earlier):
+    return lax.optimization_barrier((values, earlier))[0]
+
+
+def added(terms, start, count):
+    total = None
+    for array, base in terms:
+        piece = array[base + start : base + start + count].astype(jnp.float32)
+        total = piece if total is None else total + piece
+    return total
+
+
+def scatter_begin(keep, send):
+    arrived = swap(send, 0)
+    quarter = keep.shape[0] // 2
+    half = quarter // 2
+    parts = [[(keep, n * quarter), (arrived, n * quarter)] for n in range(2)]
+    sent = [added(terms, half, half).astype(jnp.bfloat16) for terms in parts]
+    return parts, sent, [swap(v, order[0]) for v, order in zip(sent, swap_orders())]
+
+
+def scatter_end(parts, arrived):
+    results = []
+    for terms, first, order in zip(parts, arrived, swap_orders()):
+        terms = terms + [(first, 0)]
+        half = first.shape[0]
+        for bit in order[1:]:
+            half = half // 2
+            terms.append((swap(added(terms, half, half).astype(jnp.bfloat16), bit), 0))
+        results.append(added(terms, 0, half))
+    return results
+
+
+def gather_near(parts):
+    pairs = []
     for part, order in zip(parts, swap_orders()):
         stages = order[::-1]
         for bit in stages[:-1]:
             part = jnp.concatenate([part, swap(part, bit)], axis=0)
-        pair = [part, swap(part, stages[-1])]
-        near += pair
-        far += [swap(piece, 0) for piece in pair]
-    return near + far
+        pairs.append((part, swap(part, stages[-1])))
+    return pairs
+
+
+def gather_far(pairs, *earlier):
+    far = []
+    for first, second in pairs:
+        late = after(second, *earlier) if earlier else second
+        far += [swap(first, 0), swap(late, 0)]
+    return [piece for pair in pairs for piece in pair] + far
 
 
 def shift(values, distance):
@@ -237,8 +289,8 @@
 
 def scatter_tokens(own, send):
     total = own
-    for number in range(send.shape[0]):
-        total = total + shift(send[number], number + 1).astype(jnp.float32)
+    for number, piece in enumerate(send):
+        total = total + shift(piece, number + 1).astype(jnp.float32)
     return total
 
 
@@ -267,28 +319,50 @@
     weights_two = second_blocks[0, 0]
 
     inputs_all = gather_tokens(activations)
-    cotangent_all = gather_tokens(grad_out)
-    pre_parts = scatter_sum(
-        *to_hidden(inputs_all, weights_one, model_one, target_one, col_tiles, False)
-    )
-    back_parts = scatter_sum(
-        *to_hidden(cotangent_all, weights_two, model_two, target_two, col_tiles, True)
-    )
+    cotangent_all = gather_tokens(after(grad_out, inputs_all))
+    pre_keep, pre_send = to_hidden(
+        inputs_all, weights_one, model_one, target_one, col_tiles, False
+    )
+    pre_terms, pre_sent, pre_arrived = scatter_begin(pre_keep, after(pre_send, cotangent_all))
+    back_keep, back_send = to_hidden(
+        after(cotangent_all, *pre_sent), weights_two, model_two, target_two, col_tiles, True
+    )
+    back_terms, _, back_arrived = scatter_begin(back_keep, after(back_send, *pre_arrived))
+    pre_parts = scatter_end(pre_terms, pre_arrived)
+    back_parts = scatter_end(back_terms, back_arrived)
     hidden_own, grad_pre_own = [], []
     for pre, back in zip(pre_parts, back_parts):
         hidden_full, gelu_back = jax.vjp(gelu_tanh, pre)
         hidden_own.append(hidden_full.astype(jnp.bfloat16))
         grad_pre_own.append(gelu_back(back)[0].astype(jnp.bfloat16))
-    hidden_parts = gather_parts(hidden_own)
-    grad_pre_parts = gather_parts(grad_pre_own)
+    hidden_near = gather_near(hidden_own)
+    hidden_parts = gather_far(hidden_near)
+    grad_pre_near = gather_near(after(grad_pre_own, *hidden_near))
     grad_second, own_out, send_out = to_model(
-        cotangent_all, hidden_parts, weights_two, model_two, hidden_two, live_two, members, False
-    )
-    output = scatter_tokens(own_out, send_out)
-    grad_first, own_in, send_in = to_model(
-        inputs_all, grad_pre_parts, weights_one, model_one, hidden_one, live_one, members, True
+        cotangent_all, hidden_parts, weights_two, (model_two, hidden_two, live_two), members, False
+    )
+    grad_pre_parts = gather_far(grad_pre_near, own_out)
+    output = scatter_tokens(own_out, after(send_out, *grad_pre_parts))
+    places_one = (model_one, hidden_one, live_one)
+    own_in, send_in = to_model(
+        inputs_all,
+        grad_pre_parts,
+        weights_one,
+        places_one,
+        members,
+        True,
+        with_grads=False,
     )
     grad_input = scatter_tokens(own_in, send_in)
+    (grad_first,) = to_model(
+        inputs_all,
+        after(grad_pre_parts, own_in, output),
+        weights_one,
+        places_one,
+        members,
+        True,
+        with_sums=False,
+    )
     return (output, grad_input, grad_first[None, None], grad_second[None, None])
 
 

time: 382 us -> 314 us (0.82)
  waiting for transfers between devices: 179 us -> 145 us
  starting transfers between devices: 57.2 us -> 35.6 us
  other arithmetic: 33.7 us -> 21.1 us
  Pallas kernels: 94.9 us -> 106 us
  local copies, waits for them, and re-layouts: 14.1 us -> 3.37 us
    another operation x2 -> x0, other arithmetic: 20.2 us -> none
    ppermute x12, starting transfers between devices: 37.2 us -> 18.1 us  [shift(): lax.ppermute(values, 'col', [(s, (s + distance) % count) for s in range(c...]
    ppermute x12, waiting for transfers between devices: 41 us -> 22.1 us  [shift(): lax.ppermute(values, 'col', [(s, (s + distance) % count) for s in range(c...]
    ppermute x26, waiting for transfers between devices: 138 us -> 123 us  [swap(): lax.ppermute(values, 'row', [(s, s ^ 1 << bit) for s in range(count)])]
    convert_element_type x0 -> x5, other arithmetic: none -> 11.5 us  [the longest x2 7.29 us: scatter_begin(): sent = [added(terms, half, half).astype(jnp.bfloat16) for terms in parts]]
    pallas_call x2 -> x3, Pallas kernels: 50.5 us -> 61.5 us  [to_model(): pl.pallas_call(kernel, grid_spec=pltpu.PrefetchScalarGridSpec(num_scalar_...]
    unnamed x38 -> x50, local copies, waits for them, and re-layouts: 9.05 us -> 3.19 us
    add x4 -> x2, other arithmetic: 6.49 us -> 1.81 us  [scatter_tokens(): total = total + shift(piece, number + 1).astype(jnp.float32)]
  transfers between devices with their start and end apart: 38 -> 38, of which waited for: 15 -> 17; matrix products, arithmetic and copies ran while one was open for 11% -> 5% of each run, Pallas kernels for 25% -> 34%
where the time goes in v2:
time: 314 us; the launch traced here: 312 us
  waiting for transfers between devices  145 us (46%)
  Pallas kernels  106 us (34%)
  starting transfers between devices  35.6 us (11%)
  other arithmetic  21.1 us (7%)
  local copies, waits for them, and re-layouts  3.37 us (1%)
    ppermute x26, waiting for transfers between devices, swap(): lax.ppermute(values, 'row', [(s, s ^ 1 << bit) for s in range(count)])  123 us
    pallas_call x3, Pallas kernels, to_model(): pl.pallas_call(kernel, grid_spec=pltpu.PrefetchScalarGridSpec(num_scalar_...  61.5 us
    pallas_call x2, Pallas kernels, to_hidden(): pl.pallas_call(functools.partial(to_hidden_kernel, flipped), grid_spec=pl...  44.5 us
    ppermute x12, waiting for transfers between devices, shift(): lax.ppermute(values, 'col', [(s, (s + distance) % count) for s in range(c...  22.1 us
    ppermute x12, starting transfers between devices, shift(): lax.ppermute(values, 'col', [(s, (s + distance) % count) for s in range(c...  18.1 us
    ppermute x26, starting transfers between devices, swap(): lax.ppermute(values, 'row', [(s, s ^ 1 << bit) for s in range(count)])  17.5 us
    convert_element_type x2, other arithmetic, scatter_begin(): sent = [added(terms, half, half).astype(jnp.bfloat16) for terms in parts]  7.29 us
  transfers between devices with their start and end apart: 38, of which 17 were waited for; matrix products, arithmetic and copies ran while one was open for 5% of the time, Pallas kernels for 34%

profile of v2, /device:TPU:0, one launch (start us, length us, event | category | flops | bytes accessed | tf_op | source)
XLA Modules:
  0.0 312.3 jit_solution(3136753132815587241)
XLA Ops:
  0.6 5.1 %collective-permute-start = (bf16[64,2048]{1,0:T(8,128)(2,1)}, bf16[64,2048]{1,0:T(8,128)(2,1)S(1)}, u32[]{:S(2)}, u32[]{:S(2)}) collective-permute-start(bf16[64,2048]{1,0:T(8,128)(2,1)} %param.6), channel_id=1, source_target_pairs={{0,3},{1,0},{2,1},{3,2},{4,7},{5,4},{6,5},{7,6},{8,11},{9,8},{10,9... | collective-permute-start | bytes 786440 | tf_op jit(solution)/shard_map/ppermute | solution.py:282
  9.9 2.9 collective-permute-done
  12.8 15.4 %collective-permute-done.1 = bf16[64,2048]{1,0:T(8,128)(2,1)S(1)} collective-permute-done((bf16[64,2048]{1,0:T(8,128)(2,1)}, bf16[64,2048]{1,0:T(8,128)(2,1)S(1)}, u32[]{:S(2)}, u32[]{:S(2)}) %collective-permute-start.1) | collective-permute-done | bytes 262176 | tf_op jit(solution)/shard_map/ppermute | solution.py:282
  28.4 2.8 collective-permute-start.4
  33.2 22.4 %shard_map.93 = (f32[64,256,128]{2,1,0:T(8,128)}, bf16[64,256,128]{2,1,0:T(8,128)(2,1)}) custom-call(s32[384]{0:T(512)} %get-tuple-element.87.source.refs_0_, s32[384]{0:T(512)} %get-tuple-element.74.target, bf16[256,2048]{1,0:T(8,128)(2,1)} %copy-done.7, bf16[384,128,128]{2,1,0:T(8,128)(2,1)} %bitcast.8), custom_call_target="tpu_custom_call" | custom-call | flops 12884901888 | bytes 25165824 | tf_op jit(solution)/shard_map/pallas_call | solution.py:65
  56.5 6.6 %collective-permute-done.6 = bf16[64,256,128]{2,1,0:T(8,128)(2,1)S(1)} collective-permute-done((bf16[64,256,128]{2,1,0:T(8,128)(2,1)}, bf16[64,256,128]{2,1,0:T(8,128)(2,1)S(1)}, u32[]{:S(2)}, u32[]{:S(2)}) %collective-permute-start.6) | collective-permute-done | bytes 4194336 | tf_op jit(solution)/shard_map/ppermute | solution.py:208
  63.2 4.3 %add_convert_fusion.2 = (bf16[16,256,128]{2,1,0:T(8,128)(2,1)}, bf16[16,256,128]{2,1,0:T(8,128)(2,1)}) fusion(f32[64,256,128]{2,1,0:T(8,128)} %get-tuple-element.37, bf16[64,256,128]{2,1,0:T(8,128)(2,1)S(1)} %collective-permute-done.6), kind=kLoop, calls=%fused_computation.2 | loop fusion | flops 3145728 | bytes 8388608 | tf_op jit(solution)/shard_map/convert_element_type | solution.py:246
  70.4 22.1 %shard_map.95 = (f32[64,256,128]{2,1,0:T(8,128)}, bf16[64,256,128]{2,1,0:T(8,128)(2,1)}) custom-call(s32[384]{0:T(512)} %get-tuple-element.88.refs_0_.source, s32[384]{0:T(512)} %get-tuple-element.72.target, bf16[256,2048]{1,0:T(8,128)(2,1)} %copy-done.8, bf16[384,128,128]{2,1,0:T(8,128)(2,1)} %bitcast.6), custom_call_target="tpu_custom_call" | custom-call | flops 12884901888 | bytes 25165824 | tf_op jit(solution)/shard_map/pallas_call | solution.py:65
  93.9 7.4 %collective-permute-done.19 = bf16[64,256,128]{2,1,0:T(8,128)(2,1)S(1)} collective-permute-done((bf16[64,256,128]{2,1,0:T(8,128)(2,1)}, bf16[64,256,128]{2,1,0:T(8,128)(2,1)S(1)}, u32[]{:S(2)}, u32[]{:S(2)}) %collective-permute-start.19) | collective-permute-done | bytes 4194336 | tf_op jit(solution)/shard_map/ppermute | solution.py:208
  101.3 3.0 add_convert_fusion
  109.5 32.7 %collective-permute-done.12 = bf16[8,256,128]{2,1,0:T(8,128)(2,1)S(1)} collective-permute-done((bf16[8,256,128]{2,1,0:T(8,128)(2,1)S(1)}, bf16[8,256,128]{2,1,0:T(8,128)(2,1)S(1)}, u32[]{:S(2)}, u32[]{:S(2)}) %collective-permute-start.12) | collective-permute-done | bytes 524320 | tf_op jit(solution)/shard_map/ppermute | solution.py:208
  142.2 2.4 multiply_convert_fusion
  149.2 10.3 %collective-permute-done.8 = bf16[8,256,128]{2,1,0:T(8,128)(2,1)S(1)} collective-permute-done((bf16[8,256,128]{2,1,0:T(8,128)(2,1)S(1)}, bf16[8,256,128]{2,1,0:T(8,128)(2,1)S(1)}, u32[]{:S(2)}, u32[]{:S(2)}) %collective-permute-start.8) | collective-permute-done | bytes 524320 | tf_op jit(solution)/shard_map/ppermute | solution.py:208
  160.4 8.3 %collective-permute-done.21 = bf16[8,256,128]{2,1,0:T(8,128)(2,1)S(1)} collective-permute-done((bf16[8,256,128]{2,1,0:T(8,128)(2,1)S(1)}, bf16[8,256,128]{2,1,0:T(8,128)(2,1)S(1)}, u32[]{:S(2)}, u32[]{:S(2)}) %collective-permute-start.21) | collective-permute-done | bytes 524320 | tf_op jit(solution)/shard_map/ppermute | solution.py:208
  168.7 3.6 %fusion.13 = (bf16[8,256,128]{2,1,0:T(8,128)(2,1)S(1)}, bf16[8,256,128]{2,1,0:T(8,128)(2,1)S(1)}, bf16[8,256,128]{2,1,0:T(8,128)(2,1)S(1)}) fusion(bf16[8,256,128]{2,1,0:T(8,128)(2,1)S(1)} %collective-permute-done.23, f32[64,256,128]{2,1,0:T(8,128)S(1)} %bitcast.5, bf16[16,256,128]{2,1,0:T(8,128)(2,1)S(1)} %collective-permute-done.22, ...), kind=kLoop, calls=%fused_computation.21 | loop fusion | flops 17301504 | bytes 12058624 | tf_op jit(solution)/shard_map/convert_element_type | solution.py:337
  174.6 12.7 %collective-permute-done.9 = bf16[8,256,128]{2,1,0:T(8,128)(2,1)S(1)} collective-permute-done((bf16[8,256,128]{2,1,0:T(8,128)(2,1)S(1)}, bf16[8,256,128]{2,1,0:T(8,128)(2,1)S(1)}, u32[]{:S(2)}, u32[]{:S(2)}) %collective-permute-start.9) | collective-permute-done | bytes 524320 | tf_op jit(solution)/shard_map/ppermute | solution.py:208
  187.9 19.1 %collective-permute-done.14.refs_8_ = bf16[16,256,128]{2,1,0:T(8,128)(2,1)S(1)} collective-permute-done((bf16[16,256,128]{2,1,0:T(8,128)(2,1)S(1)}, bf16[16,256,128]{2,1,0:T(8,128)(2,1)S(1)}, u32[]{:S(2)}, u32[]{:S(2)}) %collective-permute-start.14) | collective-permute-done | bytes 1048608 | tf_op jit(solution)/shard_map/ppermute | solution.py:208
  208.4 9.6 %collective-permute-done.24 = bf16[8,256,128]{2,1,0:T(8,128)(2,1)S(1)} collective-permute-done((bf16[8,256,128]{2,1,0:T(8,128)(2,1)S(1)}, bf16[8,256,128]{2,1,0:T(8,128)(2,1)S(1)}, u32[]{:S(2)}, u32[]{:S(2)}) %collective-permute-start.24) | collective-permute-done | bytes 524320 | tf_op jit(solution)/shard_map/ppermute | solution.py:208
  219.2 10.9 %collective-permute-done.26 = bf16[8,256,128]{2,1,0:T(8,128)(2,1)S(1)} collective-permute-done((bf16[8,256,128]{2,1,0:T(8,128)(2,1)S(1)}, bf16[8,256,128]{2,1,0:T(8,128)(2,1)S(1)}, u32[]{:S(2)}, u32[]{:S(2)}) %collective-permute-start.26) | collective-permute-done | bytes 524320 | tf_op jit(solution)/shard_map/ppermute | solution.py:208
  233.6 24.9 %shard_map.94 = (bf16[384,128,128]{2,1,0:T(8,128)(2,1)}, f32[64,2048]{1,0:T(8,128)}, bf16[64,2048]{1,0:T(8,128)(2,1)}, bf16[64,2048]{1,0:T(8,128)(2,1)}, bf16[64,2048]{1,0:T(8,128)(2,1)}) custom-call(s32[384]{0:T(512)} %get-tuple-element.88.refs_0_.source, s32[384]{0:T(512)} %get-tuple-element.73.refs_1_, s32[384]{0:T(512)} %convert_element_type.132.refs_2_, ...), custom_call_target="tpu_custom_call" | custom-call | flops 25769803776 | bytes 33554432 | tf_op jit(solution)/shard_map/pallas_call | solution.py:187
  265.7 18.7 %shard_map.96 = (f32[64,2048]{1,0:T(8,128)}, bf16[64,2048]{1,0:T(8,128)(2,1)}, bf16[64,2048]{1,0:T(8,128)(2,1)}, bf16[64,2048]{1,0:T(8,128)(2,1)}) custom-call(s32[384]{0:T(512)} %get-tuple-element.87.source.refs_0_, s32[384]{0:T(512)} %get-tuple-element.75.refs_1_, s32[384]{0:T(512)} %convert_element_type.172.refs_2_, bf16[384,128,128]{2,1,0:T(8,128)(2,1)} %bitcast.9, ...), custom_call_target="tpu_custom_call" | custom-call | flops 12884901888 | bytes 33554432 | tf_op jit(solution)/shard_map/pallas_call | solution.py:187
  284.4 3.3 %collective-permute-start.37 = (bf16[64,2048]{1,0:T(8,128)(2,1)}, bf16[64,2048]{1,0:T(8,128)(2,1)S(1)}, u32[]{:S(2)}, u32[]{:S(2)}) collective-permute-start(bf16[64,2048]{1,0:T(8,128)(2,1)} %get-tuple-element.58), channel_id=1, source_target_pairs={{0,3},{1,0},{2,1},{3,2},{4,7},{5,4},{6,5},{7,6},{8,11},{9,8},{10,9... | collective-permute-start | bytes 786440 | tf_op jit(solution)/shard_map/ppermute | solution.py:282
  289.8 17.9 %shard_map.97 = bf16[384,128,128]{2,1,0:T(8,128)(2,1)} custom-call(s32[384]{0:T(512)} %get-tuple-element.87.source.refs_0_, s32[384]{0:T(512)} %get-tuple-element.75.refs_1_, s32[384]{0:T(512)} %convert_element_type.172.refs_2_, bf16[256,2048]{1,0:T(8,128)(2,1)} %copy-done.7, bf16[16,256,128]{2,1,0:T(8,128)(2,1)} %copy-done.5, ...), custom_call_target="tpu_custom_call" | custom-call | flops 12884901888 | bytes 33554432 | tf_op jit(solution)/shard_map/pallas_call | solution.py:187
  307.7 3.7 %collective-permute-done.36 = bf16[64,2048]{1,0:T(8,128)(2,1)S(1)} collective-permute-done((bf16[64,2048]{1,0:T(8,128)(2,1)}, bf16[64,2048]{1,0:T(8,128)(2,1)S(1)}, u32[]{:S(2)}, u32[]{:S(2)}) %collective-permute-start.36) | collective-permute-done | bytes 262176 | tf_op jit(solution)/shard_map/ppermute | solution.py:282
  (129 shorter events, 41.0 us)
Async XLA Ops:
  28.3 27.3 %collective-permute-start.3 = (bf16[64,2048]{1,0:T(8,128)(2,1)}, bf16[64,2048]{1,0:T(8,128)(2,1)S(1)}, u32[]{:S(2)}, u32[]{:S(2)}) collective-permute-start(bf16[64,2048]{1,0:T(8,128)(2,1)} %param.7), channel_id=1, source_target_pairs={{0,3},{1,0},{2,1},{3,2},{4,7},{5,4},{6,5},{7,6},{8,11},{9,8},{10,9... | collective-permute-start | bytes 786440 | tf_op jit(solution)/shard_map/ppermute | solution.py:282
  28.4 27.2 %collective-permute-start.4 = (bf16[64,2048]{1,0:T(8,128)(2,1)}, bf16[64,2048]{1,0:T(8,128)(2,1)S(1)}, u32[]{:S(2)}, u32[]{:S(2)}) collective-permute-start(bf16[64,2048]{1,0:T(8,128)(2,1)} %param.7), channel_id=1, source_target_pairs={{0,2},{1,3},{2,0},{3,1},{4,6},{5,7},{6,4},{7,5},{8,10},{9,11},{10,... | collective-permute-start | bytes 786440 | tf_op jit(solution)/shard_map/ppermute | solution.py:282
  31.2 24.4 %collective-permute-start.5 = (bf16[64,2048]{1,0:T(8,128)(2,1)}, bf16[64,2048]{1,0:T(8,128)(2,1)S(1)}, u32[]{:S(2)}, u32[]{:S(2)}) collective-permute-start(bf16[64,2048]{1,0:T(8,128)(2,1)} %param.7), channel_id=1, source_target_pairs={{0,1},{1,2},{2,3},{3,0},{4,5},{5,6},{6,7},{7,4},{8,9},{9,10},{10,1... | collective-permute-start | bytes 786440 | tf_op jit(solution)/shard_map/ppermute | solution.py:282
  67.4 25.5 %collective-permute-start.7 = (bf16[16,256,128]{2,1,0:T(8,128)(2,1)}, bf16[16,256,128]{2,1,0:T(8,128)(2,1)}, u32[]{:S(2)}, u32[]{:S(2)}) collective-permute-start(bf16[16,256,128]{2,1,0:T(8,128)(2,1)} %get-tuple-element.86), channel_id=1, source_target_pairs={{0,8},{4,12},{8,0},{12,4},{16,24},{20,28},{24,16},{28,20},{1,9},{5... | collective-permute-start | bytes 3145736 | tf_op jit(solution)/shard_map/ppermute | solution.py:208
  68.8 25.1 %collective-permute-start.11 = (bf16[16,256,128]{2,1,0:T(8,128)(2,1)}, bf16[16,256,128]{2,1,0:T(8,128)(2,1)S(1)}, u32[]{:S(2)}, u32[]{:S(2)}) collective-permute-start(bf16[16,256,128]{2,1,0:T(8,128)(2,1)} %get-tuple-element.85), channel_id=1, source_target_pairs={{0,16},{4,20},{8,24},{12,28},{16,0},{20,4},{24,8},{28,12},{1,17},{... | collective-permute-start | bytes 3145736 | tf_op jit(solution)/shard_map/ppermute | solution.py:208
  104.3 40.7 %collective-permute-start.22 = (bf16[16,256,128]{2,1,0:T(8,128)(2,1)S(1)}, bf16[16,256,128]{2,1,0:T(8,128)(2,1)S(1)}, u32[]{:S(2)}, u32[]{:S(2)}) collective-permute-start(bf16[16,256,128]{2,1,0:T(8,128)(2,1)S(1)} %get-tuple-element.81), channel_id=1, source_target_pairs={{0,16},{4,20},{8,24},{12,28},{16,0},{20,4},{24,8},{28,12},{1,17},{... | collective-permute-start | bytes 3145736 | tf_op jit(solution)/shard_map/ppermute | solution.py:208
  106.1 39.0 %collective-permute-start.20 = (bf16[16,256,128]{2,1,0:T(8,128)(2,1)S(1)}, bf16[16,256,128]{2,1,0:T(8,128)(2,1)S(1)}, u32[]{:S(2)}, u32[]{:S(2)}) collective-permute-start(bf16[16,256,128]{2,1,0:T(8,128)(2,1)S(1)} %get-tuple-element.82), channel_id=1, source_target_pairs={{0,8},{4,12},{8,0},{12,4},{16,24},{20,28},{24,16},{28,20},{1,9},{5... | collective-permute-start | bytes 3145736 | tf_op jit(solution)/shard_map/ppermute | solution.py:208
  107.8 34.4 %collective-permute-start.12 = (bf16[8,256,128]{2,1,0:T(8,128)(2,1)S(1)}, bf16[8,256,128]{2,1,0:T(8,128)(2,1)S(1)}, u32[]{:S(2)}, u32[]{:S(2)}) collective-permute-start(bf16[8,256,128]{2,1,0:T(8,128)(2,1)S(1)} %add_convert_fusion.6), channel_id=1, source_target_pairs={{0,8},{4,12},{8,0},{12,4},{16,24},{20,28},{24,16},{28,20},{1,9},{5... | collective-permute-start | bytes 1572872 | tf_op jit(solution)/shard_map/ppermute | solution.py:208
  147.6 25.2 %collective-permute-start.13 = (bf16[8,256,128]{2,1,0:T(8,128)(2,1)S(1)}, bf16[8,256,128]{2,1,0:T(8,128)(2,1)S(1)}, u32[]{:S(2)}, u32[]{:S(2)}) collective-permute-start(bf16[8,256,128]{2,1,0:T(8,128)(2,1)S(1)} %get-tuple-element.83), channel_id=1, source_target_pairs={{0,8},{4,12},{8,0},{12,4},{16,24},{20,28},{24,16},{28,20},{1,9},{5... | collective-permute-start | bytes 1572872 | tf_op jit(solution)/shard_map/ppermute | solution.py:208
  172.9 34.0 %collective-permute-start.14 = (bf16[16,256,128]{2,1,0:T(8,128)(2,1)S(1)}, bf16[16,256,128]{2,1,0:T(8,128)(2,1)S(1)}, u32[]{:S(2)}, u32[]{:S(2)}) collective-permute-start(bf16[16,256,128]{2,1,0:T(8,128)(2,1)S(1)} %pad_maximum_fusion.1.refs_7_), channel_id=1, source_target_pairs={{0,16},{4,20},{8,24},{12,28},{16,0},{20,4},{24,8},{28,12},{1,17},{... | collective-permute-start | bytes 3145736 | tf_op jit(solution)/shard_map/ppermute | solution.py:208
  207.4 23.2 %collective-permute-start.17 = (bf16[16,256,128]{2,1,0:T(8,128)(2,1)S(1)}, bf16[16,256,128]{2,1,0:T(8,128)(2,1)S(1)}, u32[]{:S(2)}, u32[]{:S(2)}) collective-permute-start(bf16[16,256,128]{2,1,0:T(8,128)(2,1)S(1)} %pad_maximum_fusion.1.refs_7_), channel_id=1, source_target_pairs={{0,4},{4,0},{8,12},{12,8},{16,20},{20,16},{24,28},{28,24},{1,5},{5... | collective-permute-start | bytes 3145736 | tf_op jit(solution)/shard_map/ppermute | solution.py:208
  207.4 23.3 %collective-permute-start.18 = (bf16[16,256,128]{2,1,0:T(8,128)(2,1)S(1)}, bf16[16,256,128]{2,1,0:T(8,128)(2,1)S(1)}, u32[]{:S(2)}, u32[]{:S(2)}) collective-permute-start(bf16[16,256,128]{2,1,0:T(8,128)(2,1)S(1)} %collective-permute-done.14.refs_8_), channel_id=1, source_target_pairs={{0,4},{4,0},{8,12},{12,8},{16,20},{20,16},{24,28},{28,24},{1,5},{5... | collective-permute-start | bytes 3145736 | tf_op jit(solution)/shard_map/ppermute | solution.py:208
  207.9 23.6 %collective-permute-start.15 = (bf16[16,256,128]{2,1,0:T(8,128)(2,1)S(1)}, bf16[16,256,128]{2,1,0:T(8,128)(2,1)S(1)}, u32[]{:S(2)}, u32[]{:S(2)}) collective-permute-start(bf16[16,256,128]{2,1,0:T(8,128)(2,1)S(1)} %pad_maximum_fusion.refs_5_), channel_id=1, source_target_pairs={{0,4},{4,0},{8,12},{12,8},{16,20},{20,16},{24,28},{28,24},{1,5},{5... | collective-permute-start | bytes 3145736 | tf_op jit(solution)/shard_map/ppermute | solution.py:208
  207.9 23.8 %collective-permute-start.16 = (bf16[16,256,128]{2,1,0:T(8,128)(2,1)S(1)}, bf16[16,256,128]{2,1,0:T(8,128)(2,1)S(1)}, u32[]{:S(2)}, u32[]{:S(2)}) collective-permute-start(bf16[16,256,128]{2,1,0:T(8,128)(2,1)S(1)} %collective-permute-done.10.refs_6_), channel_id=1, source_target_pairs={{0,4},{4,0},{8,12},{12,8},{16,20},{20,16},{24,28},{28,24},{1,5},{5... | collective-permute-start | bytes 3145736 | tf_op jit(solution)/shard_map/ppermute | solution.py:208
  230.1 28.4 %collective-permute-start.25 = (bf16[16,256,128]{2,1,0:T(8,128)(2,1)S(1)}, bf16[16,256,128]{2,1,0:T(8,128)(2,1)S(1)}, u32[]{:S(2)}, u32[]{:S(2)}) collective-permute-start(bf16[16,256,128]{2,1,0:T(8,128)(2,1)S(1)} %constant_dynamic-update-slice_fusion.8.refs_4_), channel_id=1, source_target_pairs={{0,8},{4,12},{8,0},{12,4},{16,24},{20,28},{24,16},{28,20},{1,9},{5... | collective-permute-start | bytes 3145736 | tf_op jit(solution)/shard_map/ppermute | solution.py:208
  230.6 29.1 %collective-permute-start.28 = (bf16[16,256,128]{2,1,0:T(8,128)(2,1)S(1)}, bf16[16,256,128]{2,1,0:T(8,128)(2,1)}, u32[]{:S(2)}, u32[]{:S(2)}) collective-permute-start(bf16[16,256,128]{2,1,0:T(8,128)(2,1)S(1)} %constant_dynamic-update-slice_fusion.8.refs_4_), channel_id=1, source_target_pairs={{0,4},{4,0},{8,12},{12,8},{16,20},{20,16},{24,28},{28,24},{1,5},{5... | collective-permute-start | bytes 3145736 | tf_op jit(solution)/shard_map/ppermute | solution.py:208
  230.7 27.9 %collective-permute-start.27 = (bf16[16,256,128]{2,1,0:T(8,128)(2,1)S(1)}, bf16[16,256,128]{2,1,0:T(8,128)(2,1)}, u32[]{:S(2)}, u32[]{:S(2)}) collective-permute-start(bf16[16,256,128]{2,1,0:T(8,128)(2,1)S(1)} %constant_dynamic-update-slice_fusion.10.refs_6_), channel_id=1, source_target_pairs={{0,16},{4,20},{8,24},{12,28},{16,0},{20,4},{24,8},{28,12},{1,17},{... | collective-permute-start | bytes 3145736 | tf_op jit(solution)/shard_map/ppermute | solution.py:208
  231.5 28.3 %collective-permute-start.30 = (bf16[16,256,128]{2,1,0:T(8,128)(2,1)S(1)}, bf16[16,256,128]{2,1,0:T(8,128)(2,1)}, u32[]{:S(2)}, u32[]{:S(2)}) collective-permute-start(bf16[16,256,128]{2,1,0:T(8,128)(2,1)S(1)} %constant_dynamic-update-slice_fusion.10.refs_6_), channel_id=1, source_target_pairs={{0,4},{4,0},{8,12},{12,8},{16,20},{20,16},{24,28},{28,24},{1,5},{5... | collective-permute-start | bytes 3145736 | tf_op jit(solution)/shard_map/ppermute | solution.py:208
  263.0 25.8 %collective-permute-start.34 = (bf16[64,2048]{1,0:T(8,128)(2,1)}, bf16[64,2048]{1,0:T(8,128)(2,1)S(1)}, u32[]{:S(2)}, u32[]{:S(2)}) collective-permute-start(bf16[64,2048]{1,0:T(8,128)(2,1)} %get-tuple-element.54), channel_id=1, source_target_pairs={{0,3},{1,0},{2,1},{3,2},{4,7},{5,4},{6,5},{7,6},{8,11},{9,8},{10,9... | collective-permute-start | bytes 786440 | tf_op jit(solution)/shard_map/ppermute | solution.py:282
  265.1 23.7 %collective-permute-start.33 = (bf16[64,2048]{1,0:T(8,128)(2,1)}, bf16[64,2048]{1,0:T(8,128)(2,1)S(1)}, u32[]{:S(2)}, u32[]{:S(2)}) collective-permute-start(bf16[64,2048]{1,0:T(8,128)(2,1)} %get-tuple-element.53), channel_id=1, source_target_pairs={{0,2},{1,3},{2,0},{3,1},{4,6},{5,7},{6,4},{7,5},{8,10},{9,11},{10,... | collective-permute-start | bytes 786440 | tf_op jit(solution)/shard_map/ppermute | solution.py:282
  265.1 23.7 %collective-permute-start.32 = (bf16[64,2048]{1,0:T(8,128)(2,1)}, bf16[64,2048]{1,0:T(8,128)(2,1)S(1)}, u32[]{:S(2)}, u32[]{:S(2)}) collective-permute-start(bf16[64,2048]{1,0:T(8,128)(2,1)} %get-tuple-element.52), channel_id=1, source_target_pairs={{0,1},{1,2},{2,3},{3,0},{4,5},{5,6},{6,7},{7,4},{8,9},{9,10},{10,1... | collective-permute-start | bytes 786440 | tf_op jit(solution)/shard_map/ppermute | solution.py:282
  284.4 23.2 %collective-permute-start.37 = (bf16[64,2048]{1,0:T(8,128)(2,1)}, bf16[64,2048]{1,0:T(8,128)(2,1)S(1)}, u32[]{:S(2)}, u32[]{:S(2)}) collective-permute-start(bf16[64,2048]{1,0:T(8,128)(2,1)} %get-tuple-element.58), channel_id=1, source_target_pairs={{0,3},{1,0},{2,1},{3,2},{4,7},{5,4},{6,5},{7,6},{8,11},{9,8},{10,9... | collective-permute-start | bytes 786440 | tf_op jit(solution)/shard_map/ppermute | solution.py:282
  287.7 23.7 %collective-permute-start.36 = (bf16[64,2048]{1,0:T(8,128)(2,1)}, bf16[64,2048]{1,0:T(8,128)(2,1)S(1)}, u32[]{:S(2)}, u32[]{:S(2)}) collective-permute-start(bf16[64,2048]{1,0:T(8,128)(2,1)} %get-tuple-element.57), channel_id=1, source_target_pairs={{0,2},{1,3},{2,0},{3,1},{4,6},{5,7},{6,4},{7,5},{8,10},{9,11},{10,... | collective-permute-start | bytes 786440 | tf_op jit(solution)/shard_map/ppermute | solution.py:282
  288.8 22.5 %collective-permute-start.35 = (bf16[64,2048]{1,0:T(8,128)(2,1)}, bf16[64,2048]{1,0:T(8,128)(2,1)S(1)}, u32[]{:S(2)}, u32[]{:S(2)}) collective-permute-start(bf16[64,2048]{1,0:T(8,128)(2,1)} %get-tuple-element.56), channel_id=1, source_target_pairs={{0,1},{1,2},{2,3},{3,0},{4,5},{5,6},{6,7},{7,4},{8,9},{9,10},{10,1... | collective-permute-start | bytes 786440 | tf_op jit(solution)/shard_map/ppermute | solution.py:282
  (35 other events, 618.1 us)
